TPU v7x, 32 devices: a whole 2x2x4 slice. The times are simulated.
32 devices in a mesh: member: 8 (over y, x, core), tile: 4 (over z).
Axes of the slice: x: 2, y: 2, z: 4, core: 2. Of those that a mesh axis runs over, the one named last changes fastest.
Arguments:
- state: bfloat16 [64, 4, 32, 128], P('member', None, 'tile'), may hold values from -6 to 6
- first_weight: bfloat16 [32, 4, 3, 3], replicated, may hold values from -1 to 1
- middle_weight: bfloat16 [1, 32, 32, 3, 3], replicated, may hold values from -0.375 to 0.375
- last_weight: bfloat16 [4, 32, 3, 3], replicated, may hold values from -0.375 to 0.375
- observations: float32 [4, 8, 512], P('tile', 'member'), may hold values from -6 to 6
- obs_variance: float32 [4, 8, 512], P('tile', 'member'), may hold values from 0.5 to 4
- observation_rows: int32 [4, 8, 512], P('tile', 'member'), may hold values from 0 to 1535
- loc_class: int32 [4, 8, 512], P('tile', 'member'), may hold values from 0 to 7
Outputs:
- analysis: bfloat16 [64, 4, 32, 128], P('member', None, 'tile')
Inputs may be any that keep to these rules, and one draw needn't show every extreme that they name: `observation_rows`: each observation of patch (t, j) reads one field at one point of the patches (t - 1, j), (t, j) or (t + 1, j), tiles taken cyclically.
All inputs are finite; a program needn't handle non-finite values.
Results may differ from a plain program's by a relative error of at most 0.0054.
Values may be sent and summed in bfloat16 or wider, within the bound.
A program may use at most 128 MiB of HBM per device.

v0:
```python
import jax
import jax.numpy as jnp
from jax import lax
from jax.sharding import PartitionSpec as P

NS_ITERS = 4


def with_halo(cells, sides, width):
    for axis, dim in sides:
        count = lax.axis_size(axis)
        head = lax.slice_in_dim(cells, 0, width, axis=dim)
        tail = lax.slice_in_dim(cells, cells.shape[dim] - width, cells.shape[dim], axis=dim)
        cells = jnp.concatenate(
            [
                lax.ppermute(tail, axis, [(i, (i + 1) % count) for i in range(count)]),
                cells,
                lax.ppermute(head, axis, [((i + 1) % count, i) for i in range(count)]),
            ],
            axis=dim,
        )
    return cells


def apply_kernel_lines(padded_rows, weights):
    in_count, members_local, padded_count, width = padded_rows.shape
    out_rows = padded_count - 2
    out_count = weights.shape[0]
    stacked_taps = []
    for row_shift in range(3):
        band = padded_rows[:, :, row_shift : row_shift + out_rows, :]
        for col_shift in range(3):
            stacked_taps.append(jnp.roll(band, 1 - col_shift, axis=3))
    columns = jnp.stack(stacked_taps, axis=0).reshape(
        9 * in_count, members_local * out_rows * width
    )
    flat_weight = jnp.transpose(weights, (0, 2, 3, 1)).reshape(out_count, 9 * in_count)
    summed = jnp.dot(flat_weight, columns, preferred_element_type=jnp.float32)
    return summed.reshape(out_count, members_local, out_rows, width)


def assimilate(obs_ens, background, observed, variance, classes):
    ensemble_size = background.shape[0]
    obs_mean = jnp.mean(obs_ens, axis=1)
    obs_anom = obs_ens - obs_mean[:, None]
    obs_weight = jnp.exp(-0.25 * classes.astype(jnp.float32)) / variance
    identity = jnp.eye(ensemble_size, dtype=jnp.float32)
    highest = lax.Precision.HIGHEST
    gram = (ensemble_size - 1.0) * identity + jnp.dot(
        obs_anom.T,
        obs_weight[:, None] * obs_anom,
        precision=highest,
        preferred_element_type=jnp.float32,
    )
    norm_scale = jnp.sqrt(jnp.sum(gram * gram))
    iterate_y = gram / norm_scale
    iterate_z = identity
    for sweep in range(NS_ITERS):
        middle_factor = 1.5 * identity - 0.5 * jnp.dot(
            iterate_z, iterate_y, precision=highest, preferred_element_type=jnp.float32
        )
        iterate_y = jnp.dot(
            iterate_y, middle_factor, precision=highest, preferred_element_type=jnp.float32
        )
        iterate_z = jnp.dot(
            middle_factor, iterate_z, precision=highest, preferred_element_type=jnp.float32
        )
    root_inv = iterate_z / jnp.sqrt(norm_scale)
    measurement_residual = jnp.dot(
        obs_anom.T,
        obs_weight * (observed - obs_mean),
        precision=highest,
        preferred_element_type=jnp.float32,
    )
    mean_weights = jnp.dot(
        root_inv,
        jnp.dot(
            root_inv, measurement_residual, precision=highest, preferred_element_type=jnp.float32
        ),
        precision=highest,
        preferred_element_type=jnp.float32,
    )
    transform = jnp.sqrt(ensemble_size - 1.0) * root_inv + mean_weights[:, None]
    back = background.astype(jnp.float32)
    back_mean = jnp.mean(back, axis=0)
    back_anom = back - back_mean[None, :]
    result = back_mean[None, :] + jnp.dot(
        transform.T, back_anom, precision=highest, preferred_element_type=jnp.float32
    )
    return result.astype(jnp.bfloat16)


def analyse(neighbours, observed, variance, rows_read, classes):
    span = neighbours.shape[2]
    source_part = rows_read // span
    offset = rows_read % span
    obs_ens = neighbours[source_part, :, offset].astype(jnp.float32)
    return assimilate(obs_ens, neighbours[1], observed, variance, classes)


def local(
    state,
    first_weight,
    middle_weight,
    last_weight,
    observations,
    obs_variance,
    observation_rows,
    loc_class,
):
    patch_members, field_stack, tile_rows, width = state.shape
    depth_total = middle_weight.shape[0] + 2
    weight_list = [first_weight] + [middle_weight[0]] + [last_weight]
    feature_major_layout = jnp.transpose(state, (1, 0, 2, 3))
    hidden = with_halo(feature_major_layout, (("tile", 2),), depth_total)
    for number in range(depth_total):
        element_count = apply_kernel_lines(hidden, weight_list[number])
        if number + 1 < depth_total:
            hidden = jax.nn.silu(element_count).astype(jnp.bfloat16)
    prediction_major_layout = (feature_major_layout.astype(jnp.float32) + element_count).astype(
        jnp.bfloat16
    )
    step_member_states = jnp.transpose(prediction_major_layout, (1, 0, 2, 3))
    row_bands = lax.axis_size("member")
    points_per_patch = tile_rows // row_bands * width
    ensemble = lax.all_to_all(step_member_states, "member", split_axis=2, concat_axis=0, tiled=True)
    ensemble_size = ensemble.shape[0]
    owned = ensemble.reshape(1, ensemble_size, field_stack * points_per_patch)
    neighbours = with_halo(owned, (("tile", 0),), 1)
    analysed = analyse(
        neighbours, observations[0, 0], obs_variance[0, 0], observation_rows[0, 0], loc_class[0, 0]
    )
    outbound_values = analysed.reshape(ensemble_size, field_stack, 1, points_per_patch)
    returned = lax.all_to_all(outbound_values, "member", split_axis=0, concat_axis=2, tiled=True)
    return returned


def solution(mesh):
    return jax.shard_map(
        local,
        mesh=mesh,
        in_specs=(
            P("member", None, "tile", None),
            P(),
            P(),
            P(),
            P("tile", "member", None),
            P("tile", "member", None),
            P("tile", "member", None),
            P("tile", "member", None),
        ),
        out_specs=P("member", None, "tile", None),
        check_vma=False,
    )
```

profile of v0, /device:TPU:0, one launch (start us, length us, event | category | flops | bytes accessed | tf_op | source)
XLA Modules:
  0.0 106.4 jit_solution(1508554389513746739)
XLA Ops:
  0.0 0.9 copy.46
  0.9 3.1 %collective-permute-start = (bf16[4,8,3,128]{3,1,0,2:T(8,128)(2,1)S(1)}, bf16[4,8,3,128]{3,1,0,2:T(8,128)(2,1)S(1)}, u32[]{:S(2)}, u32[]{:S(2)}) collective-permute-start(bf16[4,8,3,128]{3,1,0,2:T(8,128)(2,1)S(1)} %get-tuple-element.41), channel_id=1, source_target_pairs={{0,1},{1,2},{2,3},{3,0},{4,5},{5,6},{6,7},{7,4},{8,9},{9,10},{10,1... | collective-permute-start | bytes 73736 | tf_op jit(solution)/shard_map/ppermute | solution.py:16
  4.0 2.1 %collective-permute-start.1 = (bf16[4,8,3,128]{3,1,0,2:T(8,128)(2,1)S(1)}, bf16[4,8,3,128]{3,1,0,2:T(8,128)(2,1)S(1)}, u32[]{:S(2)}, u32[]{:S(2)}) collective-permute-start(bf16[4,8,3,128]{3,1,0,2:T(8,128)(2,1)S(1)} %get-tuple-element.42), channel_id=1, source_target_pairs={{1,0},{2,1},{3,2},{0,3},{5,4},{6,5},{7,6},{4,7},{9,8},{10,9},{11,1... | collective-permute-start | bytes 73736 | tf_op jit(solution)/shard_map/ppermute | solution.py:18
  6.1 0.7 exponential_divide_fusion
  6.8 0.7 reshape.190
  7.5 0.9 copy.24
  8.5 0.7 copy.25
  10.9 0.6 reshape.189
  11.5 1.6 %convolution_bitcast_fusion = f32[32,12288]{1,0:T(8,128)} fusion(bf16[36,12288]{1,0:T(8,128)(2,1)S(1)} %reshape.189, bf16[32,36]{0,1:T(8,128)(2,1)S(1)} %reshape.190), kind=kOutput, calls=%fused_computation.1 | convolution fusion | flops 28311552 | bytes 2459904 | tf_op jit(solution)/shard_map/dot_general | solution.py:38
  13.1 1.8 %reshape.191 = f32[32,8,12,128]{3,2,1,0:T(8,128)S(1)} reshape(f32[32,12288]{1,0:T(8,128)} %convolution_bitcast_fusion) | data formatting | bytes 3145728 | tf_op jit(solution)/shard_map/reshape | solution.py:39
  14.9 0.6 multiply_convert_fusion.1
  15.4 1.8 %fusion.58 = (bf16[32,8,10,127]{3,2,1,0:T(8,128)(2,1)S(1)}, bf16[32,8,10,127]{3,2,1,0:T(8,128)(2,1)S(1)}, bf16[32,8,10,127]{3,2,1,0:T(8,128)(2,1)S(1)}, bf16[32,...) fusion(bf16[32,8,12,128]{3,2,1,0:T(8,128)(2,1)S(1)} %multiply_convert_fu, ...), kind=kLoop, calls=%fused_computation.124 | loop fusion | bytes 7802880 | tf_op jit(solution)/shard_map/jit(_roll_static)/slice | solution.py:33
  17.2 1.8 %fusion.59 = (bf16[32,8,10,1]{3,2,1,0:T(8,128)(2,1)S(1)}, bf16[32,8,10,1]{3,2,1,0:T(8,128)(2,1)S(1)}, bf16[32,8,10,1]{3,2,1,0:T(8,128)(2,1)S(1)}, bf16[32,8,10,1...) fusion(bf16[32,8,12,128]{3,2,1,0:T(8,128)(2,1)S(1)} %multiply_convert_fusion.1), kind=kLoop, calls=%fused_computation.125 | loop fusion | bytes 61440 | tf_op jit(solution)/shard_map/jit(_roll_static)/slice | solution.py:33
  19.1 1.6 %fusion.8 = bf16[9,32,8,10,128]{4,3,2,1,0:T(8,128)(2,1)} fusion(bf16[32,8,10,127]{3,2,1,0:T(8,128)(2,1)S(1)} %get-tuple-element.22, bf16[32,8,10,1]{3,2,1,0:T(8,128)(2,1)S(1)} %get-tuple-element.28), kind=kLoop, calls=%fused_computation.28 | loop fusion | flops 1310719 | bytes 1703936
  20.7 1.2 %fusion.7 = bf16[9,32,8,10,128]{4,3,2,1,0:T(8,128)(2,1)} fusion(bf16[9,32,8,10,128]{4,3,2,1,0:T(8,128)(2,1)} %fusion.8, bf16[32,8,12,128]{3,2,1,0:T(8,128)(2,1)S(1)} %multiply_convert_fusion.1), kind=kLoop, calls=%fused_computation.26 | loop fusion | bytes 1703936
  21.9 1.6 %fusion.9 = bf16[9,32,8,10,128]{4,3,2,1,0:T(8,128)(2,1)} fusion(bf16[9,32,8,10,128]{4,3,2,1,0:T(8,128)(2,1)} %fusion.7, bf16[32,8,10,1]{3,2,1,0:T(8,128)(2,1)S(1)} %get-tuple-element.27, bf16[32,8,10,127]{3,2,1,0:T(8,128)(2,1)S(1)} %get-tuple-element.21), kind=kLoop, calls=%fused_computation.30 | loop fusion | flops 1310720 | bytes 1703936
  23.5 1.6 %fusion.10 = bf16[9,32,8,10,128]{4,3,2,1,0:T(8,128)(2,1)} fusion(bf16[9,32,8,10,128]{4,3,2,1,0:T(8,128)(2,1)} %fusion.9, bf16[32,8,10,127]{3,2,1,0:T(8,128)(2,1)S(1)} %get-tuple-element.20, bf16[32,8,10,1]{3,2,1,0:T(8,128)(2,1)S(1)} %get-tuple-element.26), kind=kLoop, calls=%fused_computation.32 | loop fusion | flops 1310720 | bytes 1703936
  25.2 1.4 %fusion.6 = bf16[9,32,8,10,128]{4,3,2,1,0:T(8,128)(2,1)} fusion(bf16[9,32,8,10,128]{4,3,2,1,0:T(8,128)(2,1)} %fusion.10, bf16[32,8,12,128]{3,2,1,0:T(8,128)(2,1)S(1)} %multiply_convert_fusion.1), kind=kLoop, calls=%fused_computation.24 | loop fusion | bytes 1703936
  26.6 1.6 %fusion.11 = bf16[9,32,8,10,128]{4,3,2,1,0:T(8,128)(2,1)} fusion(bf16[9,32,8,10,128]{4,3,2,1,0:T(8,128)(2,1)} %fusion.6, bf16[32,8,10,1]{3,2,1,0:T(8,128)(2,1)S(1)} %get-tuple-element.25, bf16[32,8,10,127]{3,2,1,0:T(8,128)(2,1)S(1)} %get-tuple-element.19), kind=kLoop, calls=%fused_computation.34 | loop fusion | flops 1310720 | bytes 1703936
  28.3 1.6 %fusion.12 = bf16[9,32,8,10,128]{4,3,2,1,0:T(8,128)(2,1)} fusion(bf16[9,32,8,10,128]{4,3,2,1,0:T(8,128)(2,1)} %fusion.11, bf16[32,8,10,127]{3,2,1,0:T(8,128)(2,1)S(1)} %get-tuple-element.18, bf16[32,8,10,1]{3,2,1,0:T(8,128)(2,1)S(1)} %get-tuple-element.24), kind=kLoop, calls=%fused_computation.36 | loop fusion | flops 1310720 | bytes 1703936
  29.9 1.5 %fusion.5 = bf16[9,32,8,10,128]{4,3,2,1,0:T(8,128)(2,1)} fusion(bf16[9,32,8,10,128]{4,3,2,1,0:T(8,128)(2,1)} %fusion.12, bf16[32,8,12,128]{3,2,1,0:T(8,128)(2,1)S(1)} %multiply_convert_fusion.1), kind=kLoop, calls=%fused_computation.22 | loop fusion | bytes 1703936
  31.4 1.7 %fusion.13 = bf16[9,32,8,10,128]{4,3,2,1,0:T(8,128)(2,1)} fusion(bf16[9,32,8,10,128]{4,3,2,1,0:T(8,128)(2,1)} %fusion.5, bf16[32,8,10,1]{3,2,1,0:T(8,128)(2,1)S(1)} %get-tuple-element.23, bf16[32,8,10,127]{3,2,1,0:T(8,128)(2,1)S(1)} %get-tuple-element.17), kind=kLoop, calls=%fused_computation.38 | loop fusion | flops 1310720 | bytes 1703936 | tf_op jit(solution)/shard_map/stack | solution.py:34
  33.1 11.3 %reshape.192 = bf16[288,10240]{1,0:T(8,128)(2,1)} reshape(bf16[9,32,8,10,128]{4,3,2,1,0:T(8,128)(2,1)} %fusion.13) | data formatting | bytes 11796480 | tf_op jit(solution)/shard_map/reshape | solution.py:34
  44.4 3.9 %convolution_bitcast_fusion.1 = f32[32,10240]{1,0:T(8,128)S(1)} fusion(bf16[32,288]{1,0:T(8,128)(2,1)S(1)} %reshape.193, bf16[288,10240]{1,0:T(8,128)(2,1)} %reshape.192), kind=kOutput, calls=%fused_computation.2 | convolution fusion | flops 188743680 | bytes 7227392 | tf_op jit(solution)/shard_map/dot_general | solution.py:38
  48.6 0.6 multiply_convert_fusion
  49.2 0.9 fusion.56
  50.1 0.9 fusion.57
  51.0 1.1 %fusion.17 = bf16[9,32,8,8,128]{4,3,2,1,0:T(8,128)(2,1)} fusion(bf16[32,8,8,127]{3,2,1,0:T(8,128)(2,1)S(1)} %get-tuple-element.10, bf16[32,8,8,1]{3,2,1,0:T(8,128)(2,1)S(1)} %get-tuple-element.16), kind=kLoop, calls=%fused_computation.46 | loop fusion | flops 1048575 | bytes 1048576
  52.1 0.9 fusion.16
  53.0 1.1 %fusion.18 = bf16[9,32,8,8,128]{4,3,2,1,0:T(8,128)(2,1)} fusion(bf16[9,32,8,8,128]{4,3,2,1,0:T(8,128)(2,1)} %fusion.16, bf16[32,8,8,1]{3,2,1,0:T(8,128)(2,1)S(1)} %get-tuple-element.15, bf16[32,8,8,127]{3,2,1,0:T(8,128)(2,1)S(1)} %get-tuple-element.9), kind=kLoop, calls=%fused_computation.48 | loop fusion | flops 1048576 | bytes 1048576
  54.1 1.1 %fusion.19 = bf16[9,32,8,8,128]{4,3,2,1,0:T(8,128)(2,1)} fusion(bf16[9,32,8,8,128]{4,3,2,1,0:T(8,128)(2,1)} %fusion.18, bf16[32,8,8,127]{3,2,1,0:T(8,128)(2,1)S(1)} %get-tuple-element.8, bf16[32,8,8,1]{3,2,1,0:T(8,128)(2,1)S(1)} %get-tuple-element.14), kind=kLoop, calls=%fused_computation.50 | loop fusion | flops 1048576 | bytes 1048576
  55.1 1.0 fusion.15
  56.1 1.1 %fusion.20 = bf16[9,32,8,8,128]{4,3,2,1,0:T(8,128)(2,1)} fusion(bf16[9,32,8,8,128]{4,3,2,1,0:T(8,128)(2,1)} %fusion.15, bf16[32,8,8,1]{3,2,1,0:T(8,128)(2,1)S(1)} %get-tuple-element.13, bf16[32,8,8,127]{3,2,1,0:T(8,128)(2,1)S(1)} %get-tuple-element.7), kind=kLoop, calls=%fused_computation.52 | loop fusion | flops 1048576 | bytes 1048576
  57.2 1.1 %fusion.21 = bf16[9,32,8,8,128]{4,3,2,1,0:T(8,128)(2,1)} fusion(bf16[9,32,8,8,128]{4,3,2,1,0:T(8,128)(2,1)} %fusion.20, bf16[32,8,8,127]{3,2,1,0:T(8,128)(2,1)S(1)} %get-tuple-element.6, bf16[32,8,8,1]{3,2,1,0:T(8,128)(2,1)S(1)} %get-tuple-element.12), kind=kLoop, calls=%fused_computation.54 | loop fusion | flops 1048576 | bytes 1048576
  58.3 1.0 fusion.14
  59.3 1.1 %fusion.22 = bf16[9,32,8,8,128]{4,3,2,1,0:T(8,128)(2,1)} fusion(bf16[9,32,8,8,128]{4,3,2,1,0:T(8,128)(2,1)} %fusion.14, bf16[32,8,8,1]{3,2,1,0:T(8,128)(2,1)S(1)} %get-tuple-element.11, bf16[32,8,8,127]{3,2,1,0:T(8,128)(2,1)S(1)} %get-tuple-element.5), kind=kLoop, calls=%fused_computation.56 | loop fusion | flops 1048576 | bytes 1048576 | tf_op jit(solution)/shard_map/stack | solution.py:34
  60.4 8.2 %reshape.195 = bf16[288,8192]{1,0:T(8,128)(2,1)} reshape(bf16[9,32,8,8,128]{4,3,2,1,0:T(8,128)(2,1)} %fusion.22) | data formatting | bytes 9437184 | tf_op jit(solution)/shard_map/reshape | solution.py:34
  68.6 3.1 %convolution_bitcast_fusion.2 = f32[1,4,64,128]{3,1,2,0:T(4,128)S(1)} fusion(bf16[288,8192]{1,0:T(8,128)(2,1)} %reshape.195, bf16[4,288]{1,0:T(4,128)(2,1)S(1)} %reshape.196), kind=kOutput, calls=%fused_computation.5 | convolution fusion | flops 18874368 | bytes 4851968 | tf_op jit(solution)/shard_map/dot_general | solution.py:38
  71.7 0.7 fusion.41
  72.4 3.9 %all-to-all-start = ((bf16[8,4,8,128]{3,0,1,2:T(8,128)(2,1)}), bf16[8,4,8,128]{3,0,1,2:T(8,128)(2,1)S(1)}, u32[]{:S(2)}, u32[]{:S(2)}) async-start(bf16[8,4,8,128]{3,0,1,2:T(8,128)(2,1)} %fusion.41), calls=%async_computation | async-start | bytes 131072 | tf_op jit(solution)/shard_map/all_to_all | solution.py:126
  76.3 5.0 %all-to-all-done = bf16[8,4,8,128]{3,0,1,2:T(8,128)(2,1)S(1)} async-done(((bf16[8,4,8,128]{3,0,1,2:T(8,128)(2,1)}), bf16[8,4,8,128]{3,0,1,2:T(8,128)(2,1)S(1)}, u32[]{:S(2)}, u32[]{:S(2)}) %all-to-all-start) | async-done | bytes 65568 | tf_op jit(solution)/shard_map/all_to_all | solution.py:126
  81.5 3.8 %collective-permute-start.3 = (bf16[1,64,512]{1,2,0:T(8,128)(2,1)S(1)}, bf16[1,64,512]{1,2,0:T(8,128)(2,1)S(1)}, u32[]{:S(2)}, u32[]{:S(2)}) collective-permute-start(bf16[1,64,512]{1,2,0:T(8,128)(2,1)S(1)} %copy.27), channel_id=1, source_target_pairs={{1,0},{2,1},{3,2},{0,3},{5,4},{6,5},{7,6},{4,7},{9,8},{10,9},{11,1... | collective-permute-start | bytes 196616 | tf_op jit(solution)/shard_map/ppermute | solution.py:18
  85.3 4.4 %collective-permute-done.2 = bf16[1,64,512]{1,2,0:T(8,128)(2,1)S(1)} collective-permute-done((bf16[1,64,512]{1,2,0:T(8,128)(2,1)S(1)}, bf16[1,64,512]{1,2,0:T(8,128)(2,1)S(1)}, u32[]{:S(2)}, u32[]{:S(2)}) %collective-permute-start.2) | collective-permute-done | bytes 65568 | tf_op jit(solution)/shard_map/ppermute | solution.py:16
  89.8 3.2 %gather_fusion = bf16[512,64]{1,0:T(8,128)(2,1)S(1)} fusion(bf16[3,64,512]{1,2,0:T(8,128)(2,1)S(1)} %pad_maximum_fusion, s32[512]{0:T(512)S(1)} %bitcast.217), kind=kCustom, calls=%fused_computation | custom fusion | bytes 135168 | tf_op jit(solution)/shard_map/gather | solution.py:97
  93.1 1.5 %multiply_reduce_fusion = (f32[]{:T(128)}, f32[64,64]{1,0:T(8,128)S(1)}) fusion(bf16[512,64]{1,0:T(8,128)(2,1)S(1)} %gather_fusion, f32[512]{0:T(512)S(1)} %bitcast.228, f32[512]{0:T(512)S(1)} %get-tuple-element.44), kind=kOutput, calls=%fused_computation.97 | convolution fusion | flops 25350144 | bytes 86020 | tf_op jit(solution)/shard_map/dot_general | solution.py:49
  97.9 0.4 fusion
  98.3 7.4 %all_to_all.33 = bf16[64,4,1,128]{3,1,2,0:T(4,128)(2,1)S(1)} all-to-all(bf16[64,4,1,128]{3,1,2,0:T(4,128)(2,1)S(1)} %bitcast.222), channel_id=1, replica_groups=mesh['member'=8,'tile'=4] {'member'}, dimensions={0} | all-to-all | bytes 131072 | tf_op jit(solution)/shard_map/all_to_all | solution.py:134
  105.7 0.6 copy.32
  (51 shorter events, 5.0 us)
Async XLA Ops:
  0.9 8.5 %collective-permute-start = (bf16[4,8,3,128]{3,1,0,2:T(8,128)(2,1)S(1)}, bf16[4,8,3,128]{3,1,0,2:T(8,128)(2,1)S(1)}, u32[]{:S(2)}, u32[]{:S(2)}) collective-permute-start(bf16[4,8,3,128]{3,1,0,2:T(8,128)(2,1)S(1)} %get-tuple-element.41), channel_id=1, source_target_pairs={{0,1},{1,2},{2,3},{3,0},{4,5},{5,6},{6,7},{7,4},{8,9},{9,10},{10,1... | collective-permute-start | bytes 73736 | tf_op jit(solution)/shard_map/ppermute | solution.py:16
  4.0 5.4 %collective-permute-start.1 = (bf16[4,8,3,128]{3,1,0,2:T(8,128)(2,1)S(1)}, bf16[4,8,3,128]{3,1,0,2:T(8,128)(2,1)S(1)}, u32[]{:S(2)}, u32[]{:S(2)}) collective-permute-start(bf16[4,8,3,128]{3,1,0,2:T(8,128)(2,1)S(1)} %get-tuple-element.42), channel_id=1, source_target_pairs={{1,0},{2,1},{3,2},{0,3},{5,4},{6,5},{7,6},{4,7},{9,8},{10,9},{11,1... | collective-permute-start | bytes 73736 | tf_op jit(solution)/shard_map/ppermute | solution.py:18
  68.6 3.1 %copy-start = (bf16[8,4,8,128]{3,2,1,0:T(8,128)(2,1)S(1)}, bf16[8,4,8,128]{3,2,1,0:T(8,128)(2,1)}, u32[]{:S(2)}) copy-start(bf16[8,4,8,128]{3,2,1,0:T(8,128)(2,1)} %param.8) | copy-start | bytes 196612
  68.6 7.7 %copy-start.2 = (s32[1,1,512]{2,1,0:T(1,128)S(1)}, s32[1,1,512]{2,1,0:T(1,128)}, u32[]{:S(2)}) copy-start(s32[1,1,512]{2,1,0:T(1,128)} %param.14) | copy-start | bytes 6148
  68.6 24.5 %copy-start.1 = (f32[1,1,512]{2,1,0:T(1,128)S(1)}, f32[1,1,512]{2,1,0:T(1,128)}, u32[]{:S(2)}) copy-start(f32[1,1,512]{2,1,0:T(1,128)} %param.12) | copy-start | bytes 6148
  72.4 8.9 %all-to-all-start = ((bf16[8,4,8,128]{3,0,1,2:T(8,128)(2,1)}), bf16[8,4,8,128]{3,0,1,2:T(8,128)(2,1)S(1)}, u32[]{:S(2)}, u32[]{:S(2)}) async-start(bf16[8,4,8,128]{3,0,1,2:T(8,128)(2,1)} %fusion.41), calls=%async_computation | async-start | bytes 131072 | tf_op jit(solution)/shard_map/all_to_all | solution.py:126
  81.4 8.3 %collective-permute-start.2 = (bf16[1,64,512]{1,2,0:T(8,128)(2,1)S(1)}, bf16[1,64,512]{1,2,0:T(8,128)(2,1)S(1)}, u32[]{:S(2)}, u32[]{:S(2)}) collective-permute-start(bf16[1,64,512]{1,2,0:T(8,128)(2,1)S(1)} %copy.27), channel_id=1, source_target_pairs={{0,1},{1,2},{2,3},{3,0},{4,5},{5,6},{6,7},{7,4},{8,9},{9,10},{10,1... | collective-permute-start | bytes 196616 | tf_op jit(solution)/shard_map/ppermute | solution.py:16
  81.5 8.2 %collective-permute-start.3 = (bf16[1,64,512]{1,2,0:T(8,128)(2,1)S(1)}, bf16[1,64,512]{1,2,0:T(8,128)(2,1)S(1)}, u32[]{:S(2)}, u32[]{:S(2)}) collective-permute-start(bf16[1,64,512]{1,2,0:T(8,128)(2,1)S(1)} %copy.27), channel_id=1, source_target_pairs={{1,0},{2,1},{3,2},{0,3},{5,4},{6,5},{7,6},{4,7},{9,8},{10,9},{11,1... | collective-permute-start | bytes 196616 | tf_op jit(solution)/shard_map/ppermute | solution.py:18
where the time goes:
time: 107 us; the launch traced here: 106 us
  local copies, waits for them, and re-layouts  42.8 us (40%)
  other arithmetic  20 us (19%)
  starting transfers between devices  12.9 us (12%)
  matrix products  12.8 us (12%)
  waiting for transfers between devices  9.34 us (9%)
  blocking collectives  7.4 us (7%)
  between operations  1.07 us (1%)
    reshape x3, local copies, waits for them, and re-layouts, apply_kernel_lines(): jnp.stack(stacked_taps, axis=0)  20.1 us
    unnamed x15, other arithmetic  14.2 us
    dot_general x3, matrix products, apply_kernel_lines(): summed = jnp.dot(flat_weight, columns, preferred_element_type=jnp.float32)  8.51 us
    unnamed x17, local copies, waits for them, and re-layouts  7.91 us
    all_to_all x1, blocking collectives, local(): lax.all_to_all(outbound_values, 'member', split_axis=0, concat_axis=2, ti...  7.4 us
    ppermute x2, starting transfers between devices, with_halo(): lax.ppermute(head, axis, [((i + 1) % count, i) for i in range(count)])  5.9 us
    slice x6, local copies, waits for them, and re-layouts, apply_kernel_lines(): stacked_taps.append(jnp.roll(band, 1 - col_shift, axis=3))  5.75 us
    all_to_all x1, waiting for transfers between devices, local(): lax.all_to_all(step_member_states, 'member', split_axis=2, concat_axis=0,...  4.98 us
  transfers between devices with their start and end apart: 5, of which 2 were waited for; matrix products, arithmetic and copies ran while one was open for 3% of the time, Pallas kernels for 0%

commit v1 on v0

v1 whole, which is shorter than its diff:
```python
import functools

import jax
import jax.numpy as jnp
import numpy as np
from jax import lax
from jax.experimental import pallas as pl
from jax.experimental.pallas import tpu as pltpu
from jax.sharding import PartitionSpec as P

NS_ITERS = 4
MESH = pl.DeviceIdType.MESH
F32 = jnp.float32
BF16 = jnp.bfloat16
HIGHEST = lax.Precision.HIGHEST


def silu(v):
    half = 0.5 * v
    return half + half * jnp.tanh(half)


def halo_selector(fields, rows, kept):
    pick = np.zeros((2, fields, kept, fields, rows), np.float32)
    for f in range(fields):
        for q in range(kept):
            pick[0, f, q, f, rows - kept + q] = 1
            pick[1, f, q, f, q] = 1
    return pick.reshape(2 * fields * kept, fields * rows)


def first_selector(fields, rows, kept, halo, out_rows, lanes):
    where = [(f, halo - kept + q) for f in range(fields) for q in range(kept)]
    where += [(f, halo + r) for f in range(fields) for r in range(rows)]
    where += [(f, halo + rows + q) for f in range(fields) for q in range(kept)]
    count = len(where)
    spread = np.zeros((3, fields, 3, out_rows, lanes), np.float32)
    for dx in range(3):
        for k, (f, row) in enumerate(where):
            for r in range(out_rows):
                if 0 <= row - r <= 2:
                    spread[dx, f, row - r, r, dx * count + k] = 1
    return spread.reshape(9 * fields, out_rows * lanes)


def dot(a, b, precision=None):
    return jnp.dot(a, b, precision=precision, preferred_element_type=F32)


def shifted(v):
    width = v.shape[1]
    return jnp.concatenate([pltpu.roll(v, 1, 1), v, pltpu.roll(v, width - 1, 1)], axis=0)


def kernel(
    sizes,
    state_ref, pick_ref, spread_ref, first_ref, last_ref, observed_ref, variance_ref, rows_ref, class_ref, *rest,
):
    n_member, n_tile, members, fields, rows, width, channels, depth, kept, lanes = sizes
    middle = depth - 2
    middle_refs = rest[:middle]
    out_ref = rest[middle]
    taps_first = rest[middle + 1]
    taps_middle = rest[middle + 2 : middle + 2 + middle]
    (
        taps_last, onehot, halo_out, halo_in, outbox, inbox, back_out, back_in,
        halo_send, halo_recv, fore_send, fore_recv, back_send, back_recv,
    ) = rest[middle + 2 + middle :]
    me = lax.axis_index("member")
    tile = lax.axis_index("tile")
    block = fields * rows
    ensemble = n_member * members
    span = fields * width

    def tile_at(shift):
        return lax.rem(tile + shift + n_tile, n_tile)

    def member_at(shift):
        return lax.rem(me + shift, n_member)

    barrier = pltpu.get_barrier_semaphore()
    peers = [(i, d) for d in (1, -1, 0) for i in range(n_member) if (i, d) != (0, 0)]
    for i, d in peers:
        pl.semaphore_signal(barrier, inc=1, device_id=(member_at(i), tile_at(d)), device_id_type=MESH)

    for m in range(members):
        edges = dot(pick_ref[...], state_ref[m]).astype(BF16)
        half = fields * kept
        halo_out[0, m] = edges[:half]
        halo_out[1, m] = edges[half:]
    pl.semaphore_wait(barrier, len(peers))
    halo_copies = []
    for side, d in ((0, 1), (1, -1)):
        copy = pltpu.make_async_remote_copy(
            src_ref=halo_out.at[side],
            dst_ref=halo_in.at[side],
            send_sem=halo_send.at[side],
            recv_sem=halo_recv.at[side],
            device_id=(me, tile_at(d)),
            device_id_type=MESH,
        )
        copy.start()
        halo_copies.append(copy)

    with jax.named_scope("taps"):
        wide = dot(first_ref[...], spread_ref[...]).astype(BF16)
        first_rows = rows + 2 * (depth - 1)
        count = taps_first.shape[1]
        for r in range(first_rows):
            taps_first[r * channels : (r + 1) * channels, :] = wide[:, r * lanes : r * lanes + count]
        for number in range(middle):
            in_rows = rows + 2 * (depth - 1 - number)
            inner = in_rows * channels
            padded = -(-inner // 128) * 128
            base = middle_refs[number][...].astype(F32)
            base = jnp.concatenate([base, jnp.zeros((base.shape[0], padded - base.shape[1]), F32)], axis=1)
            for r in range(in_rows - 2):
                moved = (pltpu.roll(base, r * channels, 1) if r else base).astype(BF16)
                for dx in range(3):
                    taps_middle[number][r * channels : (r + 1) * channels, dx * inner : (dx + 1) * inner] = moved[
                        dx * channels : (dx + 1) * channels, :inner
                    ]
        inner = (rows + 2) * channels
        padded = -(-inner // 128) * 128
        base = last_ref[...].astype(F32)
        base = jnp.concatenate([base, jnp.zeros((base.shape[0], padded - base.shape[1]), F32)], axis=1)
        row_of = lax.rem(lax.broadcasted_iota(jnp.int32, base.shape, 0), rows)
        total = jnp.where(row_of == 0, base, 0.0)
        for r in range(1, rows):
            total = total + jnp.where(row_of == r, pltpu.roll(base, r * channels, 1), 0.0)
        taps_last[...] = total.astype(BF16)[:, :inner]

    for copy in halo_copies:
        copy.wait_recv()

    group = 2 if members % 2 == 0 else 1
    forecasts = []
    for start in range(0, members, group):
        ids = range(start, start + group)
        own = [state_ref[m].astype(F32) for m in ids]
        stacked = [
            shifted(jnp.concatenate([halo_in[0, m].astype(F32), own[g], halo_in[1, m].astype(F32)], axis=0))
            for g, m in enumerate(ids)
        ]
        hidden = silu(dot(taps_first[...], jnp.concatenate(stacked, axis=1).astype(BF16)))
        for number in range(middle):
            stacked = [shifted(hidden[:, g * width : (g + 1) * width]).astype(BF16) for g in range(group)]
            hidden = silu(dot(taps_middle[number][...], jnp.concatenate(stacked, axis=1)))
        parts = dot(taps_last[...], hidden.astype(BF16))
        for g in range(group):
            part = parts[:, g * width : (g + 1) * width]
            change = part[block : 2 * block] + pltpu.roll(part[:block], 1, 1)
            change = change + pltpu.roll(part[2 * block :], width - 1, 1)
            forecasts.append(own[g] + change)

    per_field = []
    for f in range(fields):
        cube = jnp.stack([v[f * rows : (f + 1) * rows] for v in forecasts], axis=0)
        per_field.append(jnp.transpose(cube, (1, 0, 2)))
    for r in range(rows):
        outbox[r] = jnp.concatenate([cube[r] for cube in per_field], axis=0).astype(BF16)

    fore_copies = {}
    for s in (0, 2, 1):
        for i in range(n_member):
            if s == 1 and i == 0:
                continue
            target = member_at(i)
            copy = pltpu.make_async_remote_copy(
                src_ref=outbox.at[target],
                dst_ref=inbox.at[s, me],
                send_sem=fore_send.at[s, i],
                recv_sem=fore_recv.at[s, i],
                device_id=(target, tile_at(1 - s)),
                device_id_type=MESH,
            )
            copy.start()
            fore_copies[s, i] = copy
    inbox[1, me] = outbox[me]

    read = rows_ref[...]
    spot = lax.broadcasted_iota(jnp.int32, (span, read.shape[1]), 0)
    for s in range(3):
        onehot[s] = jnp.where(spot == read - s * span, 1.0, 0.0).astype(BF16)
    obs_weight = jnp.exp(-0.25 * class_ref[...].astype(F32)) / variance_ref[...]
    eye_row = lax.broadcasted_iota(jnp.int32, (ensemble, ensemble), 0)
    eye_col = lax.broadcasted_iota(jnp.int32, (ensemble, ensemble), 1)
    identity = jnp.where(eye_row == eye_col, 1.0, 0.0).astype(F32)

    def neighbour(s):
        blocks = [inbox[s, k].astype(F32) for k in range(n_member)]
        columns = [
            jnp.concatenate([b[f * members : (f + 1) * members] for b in blocks], axis=0) for f in range(fields)
        ]
        return jnp.concatenate(columns, axis=1)

    obs_ens = None
    back = None
    for s in (1, 0, 2):
        for i in range(n_member):
            if (s, i) in fore_copies:
                fore_copies[s, i].wait_recv()
        values = neighbour(s)
        if s == 1:
            back = values
        part = dot(values.astype(BF16), onehot[s])
        obs_ens = part if obs_ens is None else obs_ens + part

    obs_mean = jnp.sum(obs_ens, axis=0, keepdims=True) / ensemble
    obs_anom = obs_ens - obs_mean
    gram = (ensemble - 1.0) * identity + lax.dot_general(
        obs_anom, obs_weight * obs_anom, (((1,), (1,)), ((), ())), precision=HIGHEST, preferred_element_type=F32
    )
    residual = jnp.sum(obs_anom * (obs_weight * (observed_ref[...] - obs_mean)), axis=1, keepdims=True)
    norm_scale = jnp.sqrt(jnp.sum(gram * gram, keepdims=True))
    iterate_y = gram / norm_scale
    iterate_z = 1.5 * identity - 0.5 * iterate_y
    iterate_y = dot(iterate_y, iterate_z, HIGHEST)
    for sweep in range(1, NS_ITERS):
        factor = 1.5 * identity - 0.5 * dot(iterate_z, iterate_y, HIGHEST)
        if sweep + 1 < NS_ITERS:
            iterate_y = dot(iterate_y, factor, HIGHEST)
        iterate_z = dot(factor, iterate_z, HIGHEST)
    root_inv = iterate_z / jnp.sqrt(norm_scale)
    back_mean = jnp.sum(back, axis=0, keepdims=True) / ensemble
    back_anom = back - back_mean
    moved = dot(root_inv, back_anom, HIGHEST)
    pull = dot(root_inv, jnp.broadcast_to(residual, (ensemble, 128)), HIGHEST)[:, :1]
    shift = back_mean + jnp.sum(pull * moved, axis=0, keepdims=True)
    analysed = shift + (ensemble - 1.0) ** 0.5 * moved

    for k in range(n_member):
        rows_k = analysed[k * members : (k + 1) * members]
        back_out[k] = jnp.concatenate(
            [rows_k[:, f * width : (f + 1) * width] for f in range(fields)], axis=0
        ).astype(BF16)
    back_copies = []
    for i in range(1, n_member):
        target = member_at(i)
        copy = pltpu.make_async_remote_copy(
            src_ref=back_out.at[target],
            dst_ref=back_in.at[me],
            send_sem=back_send.at[i],
            recv_sem=back_recv.at[i],
            device_id=(target, tile),
            device_id_type=MESH,
        )
        copy.start()
        back_copies.append(copy)
    back_in[me] = back_out[me]
    for copy in halo_copies:
        copy.wait_send()
    for copy in fore_copies.values():
        copy.wait_send()
    for copy in back_copies:
        copy.wait_recv()
    landed = [back_in[r].astype(F32) for r in range(rows)]
    per_field = []
    for f in range(fields):
        cube = jnp.stack([v[f * members : (f + 1) * members] for v in landed], axis=0)
        per_field.append(jnp.transpose(cube, (1, 0, 2)))
    for m in range(members):
        out_ref[m] = jnp.concatenate([cube[m] for cube in per_field], axis=0).astype(BF16)
    for copy in back_copies:
        copy.wait_send()


def local(state, first_weight, middle_weight, last_weight, observations, obs_variance, observation_rows, loc_class):
    members, fields, rows, width = state.shape
    channels = first_weight.shape[0]
    middle = middle_weight.shape[0]
    depth = middle + 2
    n_member = lax.axis_size("member")
    n_tile = lax.axis_size("tile")
    assert rows == n_member and n_tile >= 3
    kept = depth
    while fields * kept % 16:
        kept += 1
    assert kept <= rows
    block = fields * rows
    first_rows = rows + 2 * (depth - 1)
    count = 3 * (block + 2 * fields * kept)
    lanes = -(-count // 128) * 128
    obs = observations.shape[2]
    span = fields * width
    pick = jnp.asarray(halo_selector(fields, rows, kept), BF16)
    spread = jnp.asarray(first_selector(fields, rows, kept, depth, first_rows, lanes), BF16)
    first_taps = jnp.transpose(first_weight, (0, 3, 1, 2)).reshape(channels, 9 * fields)
    middle_taps = [
        jnp.transpose(middle_weight[n], (3, 0, 2, 1)).reshape(3 * channels, 3 * channels) for n in range(middle)
    ]
    last_taps = jnp.repeat(jnp.transpose(last_weight, (3, 0, 2, 1)).reshape(3 * fields, 3 * channels), rows, axis=0)
    sizes = (n_member, n_tile, members, fields, rows, width, channels, depth, kept, lanes)
    vmem = pl.BlockSpec(memory_space=pltpu.VMEM)
    packet = (fields * members, width)
    out = pl.pallas_call(
        functools.partial(kernel, sizes),
        out_shape=jax.ShapeDtypeStruct((members, block, width), BF16),
        in_specs=[vmem] * (9 + middle),
        out_specs=vmem,
        scratch_shapes=[
            pltpu.VMEM((first_rows * channels, count), BF16),
            *[
                pltpu.VMEM(
                    ((rows + 2 * (depth - 2 - n)) * channels, 3 * (rows + 2 * (depth - 1 - n)) * channels), BF16
                )
                for n in range(middle)
            ],
            pltpu.VMEM((3 * block, (rows + 2) * channels), BF16),
            pltpu.VMEM((3, span, obs), BF16),
            pltpu.VMEM((2, members, fields * kept, width), BF16),
            pltpu.VMEM((2, members, fields * kept, width), BF16),
            pltpu.VMEM((n_member, *packet), BF16),
            pltpu.VMEM((3, n_member, *packet), BF16),
            pltpu.VMEM((n_member, *packet), BF16),
            pltpu.VMEM((n_member, *packet), BF16),
            pltpu.SemaphoreType.DMA((2,)),
            pltpu.SemaphoreType.DMA((2,)),
            pltpu.SemaphoreType.DMA((3, n_member)),
            pltpu.SemaphoreType.DMA((3, n_member)),
            pltpu.SemaphoreType.DMA((n_member,)),
            pltpu.SemaphoreType.DMA((n_member,)),
        ],
        compiler_params=pltpu.CompilerParams(
            collective_id=0, has_side_effects=True, vmem_limit_bytes=40 * 1024 * 1024
        ),
    )(
        state.reshape(members, block, width), pick, spread, first_taps, last_taps,
        observations[0], obs_variance[0], observation_rows[0], loc_class[0], *middle_taps,
    )
    return out.reshape(members, fields, rows, width)


def solution(mesh):
    return jax.shard_map(
        local,
        mesh=mesh,
        in_specs=(
            P("member", None, "tile", None),
            P(),
            P(),
            P(),
            P("tile", "member", None),
            P("tile", "member", None),
            P("tile", "member", None),
            P("tile", "member", None),
        ),
        out_specs=P("member", None, "tile", None),
        check_vma=False,
    )
```

time: 107 us -> 29.9 us (0.28)
  local copies, waits for them, and re-layouts: 42.8 us -> 3.24 us
  Pallas kernels: 0 us -> 26.3 us
  other arithmetic: 20 us -> 0 us
  starting transfers between devices: 12.9 us -> 0 us
  matrix products: 12.8 us -> 0 us
  waiting for transfers between devices: 9.34 us -> 0 us
  blocking collectives: 7.4 us -> 0 us
    pallas_call x0 -> x1, Pallas kernels: none -> 26.3 us  [local(): pl.pallas_call(functools.partial(kernel, sizes), out_shape=jax.ShapeDtype...]
    reshape x10 -> x5, local copies, waits for them, and re-layouts: 23.3 us -> 0.32 us  [the longest x2 0.11 us: local(): jnp.transpose(first_weight, (0, 3, 1, 2)).reshape(channels, 9 * fields)]
    unnamed x15 -> x0, other arithmetic: 14.2 us -> none
    dot_general x19 -> x0, matrix products: 12.8 us -> none  [the longest x3 8.51 us: apply_kernel_lines(): summed = jnp.dot(flat_weight, columns, preferred_element_type=jnp.float32)]
    ppermute x4 -> x0, starting transfers between devices: 9.04 us -> none  [the longest x2 5.9 us: with_halo(): lax.ppermute(head, axis, [((i + 1) % count, i) for i in range(count)])]
    all_to_all x1 -> x0, blocking collectives: 7.4 us -> none  [local(): lax.all_to_all(outbound_values, 'member', split_axis=0, concat_axis=2, ti...]
    unnamed x17 -> x19, local copies, waits for them, and re-layouts: 7.91 us -> 1.93 us
    slice x7 -> x0, local copies, waits for them, and re-layouts: 5.75 us -> none  [the longest x6 5.75 us: apply_kernel_lines(): stacked_taps.append(jnp.roll(band, 1 - col_shift, axis=3))]
  transfers between devices with their start and end apart: 5 -> 0, of which waited for: 2 -> 0; matrix products, arithmetic and copies ran while one was open for 3% -> 0% of each run, Pallas kernels for 0% -> 0%
where the time goes in v1:
time: 29.9 us; the launch traced here: 29.6 us
  Pallas kernels  26.3 us (88%)
  local copies, waits for them, and re-layouts  3.24 us (11%)
    pallas_call x1, Pallas kernels, local(): pl.pallas_call(functools.partial(kernel, sizes), out_shape=jax.ShapeDtype...  26.3 us
    unnamed x19, local copies, waits for them, and re-layouts  1.93 us
    transpose x1, local copies, waits for them, and re-layouts, local(): jnp.transpose(middle_weight[n], (3, 0, 2, 1))  0.98 us

profile of v1, /device:TPU:0, one launch (start us, length us, event | category | flops | bytes accessed | tf_op | source)
XLA Modules:
  0.0 29.6 jit_solution(2272902227575428187)
XLA Ops:
  0.0 0.0 copy-start
  0.0 1.0 %copy.15 = bf16[3,32,3,32]{3,2,1,0:T(4,128)(2,1)S(1)} copy(bf16[3,32,3,32]{3,1,0,2:T(8,128)(2,1)} %bitcast.21) | data formatting | bytes 36864 | tf_op jit(solution)/shard_map/transpose | solution.py:290
  1.0 0.0 copy-start.7
  1.0 0.0 copy-start.8
  1.0 0.1 reshape.22.rest_0_
  1.1 0.6 %copy-done.7 = bf16[4,32,3,3]{1,0,3,2:T(4,128)(2,1)S(1)} copy-done((bf16[4,32,3,3]{1,0,3,2:T(4,128)(2,1)S(1)}, bf16[4,32,3,3]{1,0,3,2:T(4,128)(2,1)}, u32[]{:S(2)}) %copy-start.7) | copy-done | bytes 2328
  1.7 0.0 copy-start.1
  1.7 0.1 reshape.20
  1.8 0.0 copy-done.8
  1.8 0.0 copy-start.3
  1.8 0.0 copy-start.4
  1.9 0.0 copy-start.5
  1.9 0.0 copy-start.6
  1.9 0.1 copy.16.first_ref
  2.0 0.0 copy-start.2
  2.0 0.0 copy-done
  2.0 0.5 %copy-done.1 = bf16[8,4,8,128]{3,2,1,0:T(8,128)(2,1)S(1)} copy-done((bf16[8,4,8,128]{3,2,1,0:T(8,128)(2,1)S(1)}, bf16[8,4,8,128]{3,2,1,0:T(8,128)(2,1)}, u32[]{:S(2)}) %copy-start.1) | copy-done | bytes 65560
  2.5 0.0 copy-done.3
  2.5 0.0 copy-done.4
  2.5 0.0 copy-done.5
  2.6 0.0 copy-done.6
  2.6 0.1 copy-done.2
  2.7 26.3 %shard_map.100 = bf16[8,32,128]{2,1,0:T(8,128)(2,1)S(1)} custom-call(bf16[8,32,128]{2,1,0:T(8,128)(2,1)S(1)} %bitcast.16, bf16[32,32]{1,0:T(8,128)(2,1)S(1)} %copy-done.2, bf16[36,3072]{1,0:T(8,128)(2,1)S(1)} %copy-done, bf16[32,36]{1,0:T(8,128)(2,1)S(1)} %copy.16.first_ref, bf16[96,96]{1,0:T(8,128)(2,1)S(1)} %broadcast_bitcast_fusion.last_ref, ...), custom_call_target="tpu_custom_call" | custom-call | tf_op jit(solution)/shard_map/pallas_call | solution.py:296
  29.0 0.6 %copy.18 = bf16[8,4,8,128]{3,2,1,0:T(8,128)(2,1)} copy(bf16[8,4,8,128]{3,2,1,0:T(8,128)(2,1)S(1)} %bitcast.15) | data formatting | bytes 131072
  (4 shorter events, 0.0 us)
Async XLA Ops:
  0.0 2.0 %copy-start = (bf16[36,3072]{1,0:T(8,128)(2,1)S(1)}, bf16[36,3072]{1,0:T(8,128)(2,1)}, u32[]{:S(2)}) copy-start(bf16[36,3072]{1,0:T(8,128)(2,1)} %constant.5.clone.spread_ref) | copy-start | bytes 663556
  1.0 0.7 %copy-start.7 = (bf16[4,32,3,3]{1,0,3,2:T(4,128)(2,1)S(1)}, bf16[4,32,3,3]{1,0,3,2:T(4,128)(2,1)}, u32[]{:S(2)}) copy-start(bf16[4,32,3,3]{1,0,3,2:T(4,128)(2,1)} %param.13) | copy-start | bytes 6916
  1.0 0.8 %copy-start.8 = (bf16[32,4,3,3]{0,1,3,2:T(4,128)(2,1)S(1)}, bf16[32,4,3,3]{0,1,3,2:T(4,128)(2,1)}, u32[]{:S(2)}) copy-start(bf16[32,4,3,3]{0,1,3,2:T(4,128)(2,1)} %param.11) | copy-start | bytes 6916
  1.7 0.8 %copy-start.1 = (bf16[8,4,8,128]{3,2,1,0:T(8,128)(2,1)S(1)}, bf16[8,4,8,128]{3,2,1,0:T(8,128)(2,1)}, u32[]{:S(2)}) copy-start(bf16[8,4,8,128]{3,2,1,0:T(8,128)(2,1)} %param.10) | copy-start | bytes 196612
  1.8 0.7 %copy-start.3 = (f32[1,1,512]{2,1,0:T(1,128)S(1)}, f32[1,1,512]{2,1,0:T(1,128)}, u32[]{:S(2)}) copy-start(f32[1,1,512]{2,1,0:T(1,128)} %param.14) | copy-start | bytes 6148
  1.8 0.7 %copy-start.4 = (f32[1,1,512]{2,1,0:T(1,128)S(1)}, f32[1,1,512]{2,1,0:T(1,128)}, u32[]{:S(2)}) copy-start(f32[1,1,512]{2,1,0:T(1,128)} %param.15) | copy-start | bytes 6148
  1.9 0.7 %copy-start.5 = (s32[1,1,512]{2,1,0:T(1,128)S(1)}, s32[1,1,512]{2,1,0:T(1,128)}, u32[]{:S(2)}) copy-start(s32[1,1,512]{2,1,0:T(1,128)} %param.16) | copy-start | bytes 6148
  1.9 0.7 %copy-start.6 = (s32[1,1,512]{2,1,0:T(1,128)S(1)}, s32[1,1,512]{2,1,0:T(1,128)}, u32[]{:S(2)}) copy-start(s32[1,1,512]{2,1,0:T(1,128)} %param.17) | copy-start | bytes 6148
  2.0 0.7 %copy-start.2 = (bf16[32,32]{1,0:T(8,128)(2,1)S(1)}, bf16[32,32]{1,0:T(8,128)(2,1)}, u32[]{:S(2)}) copy-start(bf16[32,32]{1,0:T(8,128)(2,1)} %constant.4.clone.pick_ref) | copy-start | bytes 6148

commit v2 on v1

--- a/solution.py
+++ b/solution.py
@@ -12,21 +12,11 @@
 MESH = pl.DeviceIdType.MESH
 F32 = jnp.float32
 BF16 = jnp.bfloat16
-HIGHEST = lax.Precision.HIGHEST
 
 
 def silu(v):
     half = 0.5 * v
     return half + half * jnp.tanh(half)
-
-
-def halo_selector(fields, rows, kept):
-    pick = np.zeros((2, fields, kept, fields, rows), np.float32)
-    for f in range(fields):
-        for q in range(kept):
-            pick[0, f, q, f, rows - kept + q] = 1
-            pick[1, f, q, f, q] = 1
-    return pick.reshape(2 * fields * kept, fields * rows)
 
 
 def first_selector(fields, rows, kept, halo, out_rows, lanes):
@@ -34,17 +24,28 @@
     where += [(f, halo + r) for f in range(fields) for r in range(rows)]
     where += [(f, halo + rows + q) for f in range(fields) for q in range(kept)]
     count = len(where)
-    spread = np.zeros((3, fields, 3, out_rows, lanes), np.float32)
+    spread = np.zeros((3, 3, fields, out_rows, lanes), np.float32)
     for dx in range(3):
         for k, (f, row) in enumerate(where):
             for r in range(out_rows):
                 if 0 <= row - r <= 2:
-                    spread[dx, f, row - r, r, dx * count + k] = 1
+                    spread[row - r, dx, f, r, dx * count + k] = 1
     return spread.reshape(9 * fields, out_rows * lanes)
 
 
-def dot(a, b, precision=None):
-    return jnp.dot(a, b, precision=precision, preferred_element_type=F32)
+def dot(a, b):
+    return jnp.dot(a, b, preferred_element_type=F32)
+
+
+def split(v):
+    high = v.astype(BF16)
+    return high, (v - high.astype(F32)).astype(BF16)
+
+
+def dot_split(a, b):
+    a_high, a_low = split(a)
+    b_high, b_low = split(b)
+    return dot(jnp.concatenate([a_high, a_low, a_high], axis=1), jnp.concatenate([b_high, b_high, b_low], axis=0))
 
 
 def shifted(v):
@@ -52,20 +53,33 @@
     return jnp.concatenate([pltpu.roll(v, 1, 1), v, pltpu.roll(v, width - 1, 1)], axis=0)
 
 
-def kernel(
-    sizes,
-    state_ref, pick_ref, spread_ref, first_ref, last_ref, observed_ref, variance_ref, rows_ref, class_ref, *rest,
-):
+def tap_rows(load, padded):
+    lines = []
+    for dx in range(3):
+        parts = [load(3 * dy + dx) for dy in range(3)]
+        filler = jnp.zeros((parts[0].shape[0], padded - 3 * parts[0].shape[1]), F32)
+        lines.append(jnp.concatenate([*parts, filler], axis=1))
+    return jnp.concatenate(lines, axis=0)
+
+
+def kernel(sizes, *refs):
     n_member, n_tile, members, fields, rows, width, channels, depth, kept, lanes = sizes
     middle = depth - 2
-    middle_refs = rest[:middle]
-    out_ref = rest[middle]
-    taps_first = rest[middle + 1]
-    taps_middle = rest[middle + 2 : middle + 2 + middle]
+    sources, out_ref, refs = refs[:9], refs[9], refs[10:]
+    fetched, refs = refs[:9], refs[9:]
     (
-        taps_last, onehot, halo_out, halo_in, outbox, inbox, back_out, back_in,
+        state_ref, spread_ref, first_ref, middle_ref, last_ref, observed_ref, variance_ref, rows_ref, class_ref,
+    ) = fetched
+    taps_first, taps_middle, refs = refs[0], refs[1 : 1 + middle], refs[1 + middle :]
+    (
+        taps_last, onehot, halo_out, halo_in, outbox, inbox, back_out, back_in, fetch_sem,
         halo_send, halo_recv, fore_send, fore_recv, back_send, back_recv,
-    ) = rest[middle + 2 + middle :]
+    ) = refs
+    fetches = [
+        pltpu.make_async_copy(source, target, fetch_sem.at[n])
+        for n, (source, target) in enumerate(zip(sources, fetched))
+    ]
+    fetches[0].start()
     me = lax.axis_index("member")
     tile = lax.axis_index("tile")
     block = fields * rows
@@ -83,11 +97,14 @@
     for i, d in peers:
         pl.semaphore_signal(barrier, inc=1, device_id=(member_at(i), tile_at(d)), device_id_type=MESH)
 
+    for fetch in fetches[1:]:
+        fetch.start()
+    fetches[0].wait()
     for m in range(members):
-        edges = dot(pick_ref[...], state_ref[m]).astype(BF16)
-        half = fields * kept
-        halo_out[0, m] = edges[:half]
-        halo_out[1, m] = edges[half:]
+        whole = state_ref[m].astype(F32)
+        each = [whole[f * rows : (f + 1) * rows] for f in range(fields)]
+        halo_out[0, m] = jnp.concatenate([v[rows - kept :] for v in each], axis=0).astype(BF16)
+        halo_out[1, m] = jnp.concatenate([v[:kept] for v in each], axis=0).astype(BF16)
     pl.semaphore_wait(barrier, len(peers))
     halo_copies = []
     for side, d in ((0, 1), (1, -1)):
@@ -103,7 +120,12 @@
         halo_copies.append(copy)
 
     with jax.named_scope("taps"):
-        wide = dot(first_ref[...], spread_ref[...]).astype(BF16)
+        for fetch in fetches[1:]:
+            fetch.wait()
+        first_taps = jnp.concatenate([first_ref[n].astype(F32) for n in range(9)], axis=0).astype(BF16)
+        wide = lax.dot_general(
+            first_taps, spread_ref[...], (((0,), (0,)), ((), ())), preferred_element_type=F32
+        ).astype(BF16)
         first_rows = rows + 2 * (depth - 1)
         count = taps_first.shape[1]
         for r in range(first_rows):
@@ -112,8 +134,7 @@
             in_rows = rows + 2 * (depth - 1 - number)
             inner = in_rows * channels
             padded = -(-inner // 128) * 128
-            base = middle_refs[number][...].astype(F32)
-            base = jnp.concatenate([base, jnp.zeros((base.shape[0], padded - base.shape[1]), F32)], axis=1)
+            base = tap_rows(lambda n: middle_ref[9 * number + n].astype(F32), padded)
             for r in range(in_rows - 2):
                 moved = (pltpu.roll(base, r * channels, 1) if r else base).astype(BF16)
                 for dx in range(3):
@@ -122,8 +143,8 @@
                     ]
         inner = (rows + 2) * channels
         padded = -(-inner // 128) * 128
-        base = last_ref[...].astype(F32)
-        base = jnp.concatenate([base, jnp.zeros((base.shape[0], padded - base.shape[1]), F32)], axis=1)
+        base = tap_rows(lambda n: last_ref[n].astype(F32), padded)
+        base = jnp.broadcast_to(base[:, None, :], (base.shape[0], rows, padded)).reshape(-1, padded)
         row_of = lax.rem(lax.broadcasted_iota(jnp.int32, base.shape, 0), rows)
         total = jnp.where(row_of == 0, base, 0.0)
         for r in range(1, rows):
@@ -208,24 +229,29 @@
 
     obs_mean = jnp.sum(obs_ens, axis=0, keepdims=True) / ensemble
     obs_anom = obs_ens - obs_mean
+    anom_high, anom_low = split(obs_anom)
+    heavy_high, heavy_low = split(obs_weight * obs_anom)
     gram = (ensemble - 1.0) * identity + lax.dot_general(
-        obs_anom, obs_weight * obs_anom, (((1,), (1,)), ((), ())), precision=HIGHEST, preferred_element_type=F32
+        jnp.concatenate([anom_high, anom_low, anom_high], axis=1),
+        jnp.concatenate([heavy_high, heavy_high, heavy_low], axis=1),
+        (((1,), (1,)), ((), ())),
+        preferred_element_type=F32,
     )
     residual = jnp.sum(obs_anom * (obs_weight * (observed_ref[...] - obs_mean)), axis=1, keepdims=True)
     norm_scale = jnp.sqrt(jnp.sum(gram * gram, keepdims=True))
     iterate_y = gram / norm_scale
     iterate_z = 1.5 * identity - 0.5 * iterate_y
-    iterate_y = dot(iterate_y, iterate_z, HIGHEST)
+    iterate_y = dot_split(iterate_y, iterate_z)
     for sweep in range(1, NS_ITERS):
-        factor = 1.5 * identity - 0.5 * dot(iterate_z, iterate_y, HIGHEST)
+        factor = 1.5 * identity - 0.5 * dot_split(iterate_z, iterate_y)
         if sweep + 1 < NS_ITERS:
-            iterate_y = dot(iterate_y, factor, HIGHEST)
-        iterate_z = dot(factor, iterate_z, HIGHEST)
+            iterate_y = dot_split(iterate_y, factor)
+        iterate_z = dot_split(factor, iterate_z)
     root_inv = iterate_z / jnp.sqrt(norm_scale)
     back_mean = jnp.sum(back, axis=0, keepdims=True) / ensemble
     back_anom = back - back_mean
-    moved = dot(root_inv, back_anom, HIGHEST)
-    pull = dot(root_inv, jnp.broadcast_to(residual, (ensemble, 128)), HIGHEST)[:, :1]
+    both = dot_split(root_inv, jnp.concatenate([back_anom, jnp.broadcast_to(residual, (ensemble, 128))], axis=1))
+    moved, pull = both[:, :span], both[:, span : span + 1]
     shift = back_mean + jnp.sum(pull * moved, axis=0, keepdims=True)
     analysed = shift + (ensemble - 1.0) ** 0.5 * moved
 
@@ -283,22 +309,28 @@
     lanes = -(-count // 128) * 128
     obs = observations.shape[2]
     span = fields * width
-    pick = jnp.asarray(halo_selector(fields, rows, kept), BF16)
     spread = jnp.asarray(first_selector(fields, rows, kept, depth, first_rows, lanes), BF16)
-    first_taps = jnp.transpose(first_weight, (0, 3, 1, 2)).reshape(channels, 9 * fields)
-    middle_taps = [
-        jnp.transpose(middle_weight[n], (3, 0, 2, 1)).reshape(3 * channels, 3 * channels) for n in range(middle)
-    ]
-    last_taps = jnp.repeat(jnp.transpose(last_weight, (3, 0, 2, 1)).reshape(3 * fields, 3 * channels), rows, axis=0)
+    operands = (
+        state.reshape(members, block, width),
+        spread,
+        jnp.transpose(first_weight, (2, 3, 1, 0)).reshape(9, fields, channels),
+        jnp.transpose(middle_weight, (0, 3, 4, 1, 2)).reshape(9 * middle, channels, channels),
+        jnp.transpose(last_weight, (2, 3, 0, 1)).reshape(9, fields, channels),
+        observations[0],
+        obs_variance[0],
+        observation_rows[0],
+        loc_class[0],
+    )
     sizes = (n_member, n_tile, members, fields, rows, width, channels, depth, kept, lanes)
     vmem = pl.BlockSpec(memory_space=pltpu.VMEM)
     packet = (fields * members, width)
     out = pl.pallas_call(
         functools.partial(kernel, sizes),
         out_shape=jax.ShapeDtypeStruct((members, block, width), BF16),
-        in_specs=[vmem] * (9 + middle),
+        in_specs=[pl.BlockSpec(memory_space=pltpu.HBM)] * len(operands),
         out_specs=vmem,
         scratch_shapes=[
+            *[pltpu.VMEM(v.shape, v.dtype) for v in operands],
             pltpu.VMEM((first_rows * channels, count), BF16),
             *[
                 pltpu.VMEM(
@@ -314,6 +346,7 @@
             pltpu.VMEM((3, n_member, *packet), BF16),
             pltpu.VMEM((n_member, *packet), BF16),
             pltpu.VMEM((n_member, *packet), BF16),
+            pltpu.SemaphoreType.DMA((len(operands),)),
             pltpu.SemaphoreType.DMA((2,)),
             pltpu.SemaphoreType.DMA((2,)),
             pltpu.SemaphoreType.DMA((3, n_member)),
@@ -322,12 +355,9 @@
             pltpu.SemaphoreType.DMA((n_member,)),
         ],
         compiler_params=pltpu.CompilerParams(
-            collective_id=0, has_side_effects=True, vmem_limit_bytes=40 * 1024 * 1024
+            collective_id=0, has_side_effects=True, vmem_limit_bytes=60 * 1024 * 1024
         ),
-    )(
-        state.reshape(members, block, width), pick, spread, first_taps, last_taps,
-        observations[0], obs_variance[0], observation_rows[0], loc_class[0], *middle_taps,
-    )
+    )(*operands)
     return out.reshape(members, fields, rows, width)
 
 

time: 29.9 us -> 28.6 us (0.957)
  local copies, waits for them, and re-layouts: 3.24 us -> 1.47 us
  Pallas kernels: 26.3 us -> 26.9 us
    transpose x3 -> x0, local copies, waits for them, and re-layouts: 0.99 us -> none  [the longest x1 0.98 us: local(): jnp.transpose(middle_weight[n], (3, 0, 2, 1))]
    pallas_call x1, Pallas kernels: 26.3 us -> 26.9 us  [local(): pl.pallas_call(functools.partial(kernel, sizes), out_shape=jax.ShapeDtype...]
    unnamed x19 -> x1, local copies, waits for them, and re-layouts: 1.93 us -> 1.47 us
    reshape x5 -> x0, local copies, waits for them, and re-layouts: 0.32 us -> none  [the longest x2 0.11 us: local(): jnp.transpose(first_weight, (0, 3, 1, 2)).reshape(channels, 9 * fields)]
where the time goes in v2:
time: 28.6 us; the launch traced here: 28.4 us
  Pallas kernels  26.9 us (94%)
  local copies, waits for them, and re-layouts  1.47 us (5%)
    pallas_call x1, Pallas kernels, local(): pl.pallas_call(functools.partial(kernel, sizes), out_shape=jax.ShapeDtype...  26.9 us
    unnamed x1, local copies, waits for them, and re-layouts  1.47 us

profile of v2, /device:TPU:0, one launch (start us, length us, event | category | flops | bytes accessed | tf_op | source)
XLA Modules:
  0.0 28.4 jit_solution(16084800388269320137)
XLA Ops:
  0.0 26.9 %shard_map.91 = bf16[8,32,128]{2,1,0:T(8,128)(2,1)} custom-call(bf16[8,32,128]{2,1,0:T(8,128)(2,1)} %bitcast.17, bf16[36,3072]{1,0:T(8,128)(2,1)} %constant.2.clone.refs_1_, bf16[9,4,32]{2,1,0:T(4,128)(2,1)} %bitcast.18, bf16[9,32,32]{2,1,0:T(8,128)(2,1)} %bitcast.16, bf16[9,4,32]{2,1,0:T(4,128)(2,1)} %bitcast.19, f32[1,512]{1,0:T(1,128)} %bitcast.20, ...), custom_call_target="tpu_custom_call" | custom-call | tf_op jit(solution)/shard_map/pallas_call | solution.py:327
  26.9 1.5 %copy.11 = bf16[8,4,8,128]{3,2,1,0:T(8,128)(2,1)} copy(bf16[8,4,8,128]{3,2,1,0:T(8,128)(2,1)} %bitcast.15) | data formatting | bytes 131072

commit v3 on v2

--- a/solution.py
+++ b/solution.py
@@ -63,7 +63,7 @@
 
 
 def kernel(sizes, *refs):
-    n_member, n_tile, members, fields, rows, width, channels, depth, kept, lanes = sizes
+    n_member, n_tile, members, fields, rows, width, channels, depth, kept, lanes, halves = sizes
     middle = depth - 2
     sources, out_ref, refs = refs[:9], refs[9], refs[10:]
     fetched, refs = refs[:9], refs[9:]
@@ -154,50 +154,52 @@
     for copy in halo_copies:
         copy.wait_recv()
 
-    group = 2 if members % 2 == 0 else 1
-    forecasts = []
-    for start in range(0, members, group):
-        ids = range(start, start + group)
-        own = [state_ref[m].astype(F32) for m in ids]
-        stacked = [
-            shifted(jnp.concatenate([halo_in[0, m].astype(F32), own[g], halo_in[1, m].astype(F32)], axis=0))
-            for g, m in enumerate(ids)
-        ]
-        hidden = silu(dot(taps_first[...], jnp.concatenate(stacked, axis=1).astype(BF16)))
-        for number in range(middle):
-            stacked = [shifted(hidden[:, g * width : (g + 1) * width]).astype(BF16) for g in range(group)]
-            hidden = silu(dot(taps_middle[number][...], jnp.concatenate(stacked, axis=1)))
-        parts = dot(taps_last[...], hidden.astype(BF16))
-        for g in range(group):
-            part = parts[:, g * width : (g + 1) * width]
-            change = part[block : 2 * block] + pltpu.roll(part[:block], 1, 1)
-            change = change + pltpu.roll(part[2 * block :], width - 1, 1)
-            forecasts.append(own[g] + change)
-
-    per_field = []
-    for f in range(fields):
-        cube = jnp.stack([v[f * rows : (f + 1) * rows] for v in forecasts], axis=0)
-        per_field.append(jnp.transpose(cube, (1, 0, 2)))
-    for r in range(rows):
-        outbox[r] = jnp.concatenate([cube[r] for cube in per_field], axis=0).astype(BF16)
-
+    share = members // halves
+    group = 2 if share % 2 == 0 else 1
     fore_copies = {}
-    for s in (0, 2, 1):
-        for i in range(n_member):
-            if s == 1 and i == 0:
-                continue
-            target = member_at(i)
-            copy = pltpu.make_async_remote_copy(
-                src_ref=outbox.at[target],
-                dst_ref=inbox.at[s, me],
-                send_sem=fore_send.at[s, i],
-                recv_sem=fore_recv.at[s, i],
-                device_id=(target, tile_at(1 - s)),
-                device_id_type=MESH,
-            )
-            copy.start()
-            fore_copies[s, i] = copy
-    inbox[1, me] = outbox[me]
+    for half in range(halves):
+        forecasts = []
+        for start in range(half * share, (half + 1) * share, group):
+            ids = range(start, start + group)
+            own = [state_ref[m].astype(F32) for m in ids]
+            stacked = [
+                shifted(jnp.concatenate([halo_in[0, m].astype(F32), own[g], halo_in[1, m].astype(F32)], axis=0))
+                for g, m in enumerate(ids)
+            ]
+            hidden = silu(dot(taps_first[...], jnp.concatenate(stacked, axis=1).astype(BF16)))
+            for number in range(middle):
+                stacked = [shifted(hidden[:, g * width : (g + 1) * width]).astype(BF16) for g in range(group)]
+                hidden = silu(dot(taps_middle[number][...], jnp.concatenate(stacked, axis=1)))
+            parts = dot(taps_last[...], hidden.astype(BF16))
+            for g in range(group):
+                part = parts[:, g * width : (g + 1) * width]
+                change = part[block : 2 * block] + pltpu.roll(part[:block], 1, 1)
+                change = change + pltpu.roll(part[2 * block :], width - 1, 1)
+                forecasts.append(own[g] + change)
+
+        per_field = []
+        for f in range(fields):
+            cube = jnp.stack([v[f * rows : (f + 1) * rows] for v in forecasts], axis=0)
+            per_field.append(jnp.transpose(cube, (1, 0, 2)))
+        for r in range(rows):
+            outbox[half, r] = jnp.concatenate([cube[r] for cube in per_field], axis=0).astype(BF16)
+
+        for s in (0, 2, 1):
+            for i in range(n_member):
+                if s == 1 and i == 0:
+                    continue
+                target = member_at(i)
+                copy = pltpu.make_async_remote_copy(
+                    src_ref=outbox.at[half, target],
+                    dst_ref=inbox.at[s, half, me],
+                    send_sem=fore_send.at[s, half, i],
+                    recv_sem=fore_recv.at[s, half, i],
+                    device_id=(target, tile_at(1 - s)),
+                    device_id_type=MESH,
+                )
+                copy.start()
+                fore_copies[s, half, i] = copy
+        inbox[1, half, me] = outbox[half, me]
 
     read = rows_ref[...]
     spot = lax.broadcasted_iota(jnp.int32, (span, read.shape[1]), 0)
@@ -209,18 +211,19 @@
     identity = jnp.where(eye_row == eye_col, 1.0, 0.0).astype(F32)
 
     def neighbour(s):
-        blocks = [inbox[s, k].astype(F32) for k in range(n_member)]
+        blocks = [inbox[s, half, k].astype(F32) for k in range(n_member) for half in range(halves)]
         columns = [
-            jnp.concatenate([b[f * members : (f + 1) * members] for b in blocks], axis=0) for f in range(fields)
+            jnp.concatenate([b[f * share : (f + 1) * share] for b in blocks], axis=0) for f in range(fields)
         ]
         return jnp.concatenate(columns, axis=1)
 
     obs_ens = None
     back = None
     for s in (1, 0, 2):
-        for i in range(n_member):
-            if (s, i) in fore_copies:
-                fore_copies[s, i].wait_recv()
+        for half in range(halves):
+            for i in range(n_member):
+                if (s, half, i) in fore_copies:
+                    fore_copies[s, half, i].wait_recv()
         values = neighbour(s)
         if s == 1:
             back = values
@@ -321,12 +324,13 @@
         observation_rows[0],
         loc_class[0],
     )
-    sizes = (n_member, n_tile, members, fields, rows, width, channels, depth, kept, lanes)
+    halves = 2 if members % 2 == 0 and (fields * members // 2) % 16 == 0 else 1
+    sizes = (n_member, n_tile, members, fields, rows, width, channels, depth, kept, lanes, halves)
     vmem = pl.BlockSpec(memory_space=pltpu.VMEM)
     packet = (fields * members, width)
     out = pl.pallas_call(
         functools.partial(kernel, sizes),
-        out_shape=jax.ShapeDtypeStruct((members, block, width), BF16),
+        out_shape=pltpu.VMEM((members, block, width), BF16),
         in_specs=[pl.BlockSpec(memory_space=pltpu.HBM)] * len(operands),
         out_specs=vmem,
         scratch_shapes=[
@@ -342,15 +346,15 @@
             pltpu.VMEM((3, span, obs), BF16),
             pltpu.VMEM((2, members, fields * kept, width), BF16),
             pltpu.VMEM((2, members, fields * kept, width), BF16),
-            pltpu.VMEM((n_member, *packet), BF16),
-            pltpu.VMEM((3, n_member, *packet), BF16),
+            pltpu.VMEM((halves, n_member, fields * members // halves, width), BF16),
+            pltpu.VMEM((3, halves, n_member, fields * members // halves, width), BF16),
             pltpu.VMEM((n_member, *packet), BF16),
             pltpu.VMEM((n_member, *packet), BF16),
             pltpu.SemaphoreType.DMA((len(operands),)),
             pltpu.SemaphoreType.DMA((2,)),
             pltpu.SemaphoreType.DMA((2,)),
-            pltpu.SemaphoreType.DMA((3, n_member)),
-            pltpu.SemaphoreType.DMA((3, n_member)),
+            pltpu.SemaphoreType.DMA((3, halves, n_member)),
+            pltpu.SemaphoreType.DMA((3, halves, n_member)),
             pltpu.SemaphoreType.DMA((n_member,)),
             pltpu.SemaphoreType.DMA((n_member,)),
         ],

time: 28.6 us -> 27.6 us (0.965)
  local copies, waits for them, and re-layouts: 1.47 us -> 0.63 us
    unnamed x1, local copies, waits for them, and re-layouts: 1.47 us -> 0.63 us
where the time goes in v3:
time: 27.6 us; the launch traced here: 27.5 us
  Pallas kernels  26.8 us (97%)
  local copies, waits for them, and re-layouts  0.63 us (2%)
    pallas_call x1, Pallas kernels, local(): pl.pallas_call(functools.partial(kernel, sizes), out_shape=pltpu.VMEM((me...  26.8 us
    unnamed x1, local copies, waits for them, and re-layouts  0.63 us

profile of v3, /device:TPU:0, one launch (start us, length us, event | category | flops | bytes accessed | tf_op | source)
XLA Modules:
  0.0 27.5 jit_solution(16561135228457370410)
XLA Ops:
  0.0 26.8 %shard_map.91 = bf16[8,32,128]{2,1,0:T(8,128)(2,1)S(1)} custom-call(bf16[8,32,128]{2,1,0:T(8,128)(2,1)} %bitcast.17, bf16[36,3072]{1,0:T(8,128)(2,1)} %constant.2.clone.refs_1_, bf16[9,4,32]{2,1,0:T(4,128)(2,1)} %bitcast.18, bf16[9,32,32]{2,1,0:T(8,128)(2,1)} %bitcast.16, bf16[9,4,32]{2,1,0:T(4,128)(2,1)} %bitcast.19, f32[1,512]{1,0:T(1,128)} %bitcast.20, ...), custom_call_target="tpu_custom_call" | custom-call | tf_op jit(solution)/shard_map/pallas_call | solution.py:331
  26.8 0.6 %copy.11 = bf16[8,4,8,128]{3,2,1,0:T(8,128)(2,1)} copy(bf16[8,4,8,128]{3,2,1,0:T(8,128)(2,1)S(1)} %bitcast.15) | data formatting | bytes 131072

commit v4 on v3

--- a/solution.py
+++ b/solution.py
@@ -42,15 +42,28 @@
     return high, (v - high.astype(F32)).astype(BF16)
 
 
-def dot_split(a, b):
-    a_high, a_low = split(a)
+def dot_split(a_twice, b):
+    high, low = split(a_twice)
+    size = a_twice.shape[0]
+    lane = lax.broadcasted_iota(jnp.int32, a_twice.shape, 1)
+    mixed = jnp.where(lane < size, high.astype(F32), low.astype(F32)).astype(BF16)
     b_high, b_low = split(b)
-    return dot(jnp.concatenate([a_high, a_low, a_high], axis=1), jnp.concatenate([b_high, b_high, b_low], axis=0))
+    return dot(jnp.concatenate([mixed, mixed], axis=1), jnp.concatenate([b_high, b_high, b_low, b_low], axis=0))
 
 
 def shifted(v):
     width = v.shape[1]
     return jnp.concatenate([pltpu.roll(v, 1, 1), v, pltpu.roll(v, width - 1, 1)], axis=0)
+
+
+def gathered(parts, width):
+    third = parts.shape[0] // 3
+    sums = []
+    for at in range(0, parts.shape[1], width):
+        part = parts[:, at : at + width]
+        left, right = pltpu.roll(part[:third], 1, 1), pltpu.roll(part[2 * third :], width - 1, 1)
+        sums.append(part[third : 2 * third] + left + right)
+    return jnp.concatenate(sums, axis=1)
 
 
 def tap_rows(load, padded):
@@ -63,7 +76,7 @@
 
 
 def kernel(sizes, *refs):
-    n_member, n_tile, members, fields, rows, width, channels, depth, kept, lanes, halves = sizes
+    n_member, n_tile, members, fields, rows, width, channels, depth, kept, lanes, halves, chunks = sizes
     middle = depth - 2
     sources, out_ref, refs = refs[:9], refs[9], refs[10:]
     fetched, refs = refs[:9], refs[9:]
@@ -86,11 +99,15 @@
     ensemble = n_member * members
     span = fields * width
 
+    def wrapped(index, count):
+        index = jnp.where(index >= count, index - count, index)
+        return jnp.where(index < 0, index + count, index)
+
     def tile_at(shift):
-        return lax.rem(tile + shift + n_tile, n_tile)
+        return wrapped(tile + shift, n_tile) if shift else tile
 
     def member_at(shift):
-        return lax.rem(me + shift, n_member)
+        return wrapped(me + shift, n_member) if shift else me
 
     barrier = pltpu.get_barrier_semaphore()
     peers = [(i, d) for d in (1, -1, 0) for i in range(n_member) if (i, d) != (0, 0)]
@@ -131,16 +148,15 @@
         for r in range(first_rows):
             taps_first[r * channels : (r + 1) * channels, :] = wide[:, r * lanes : r * lanes + count]
         for number in range(middle):
-            in_rows = rows + 2 * (depth - 1 - number)
-            inner = in_rows * channels
+            chunk = chunks[number]
+            inner = (chunk + 2) * channels
             padded = -(-inner // 128) * 128
             base = tap_rows(lambda n: middle_ref[9 * number + n].astype(F32), padded)
-            for r in range(in_rows - 2):
+            for r in range(chunk):
                 moved = (pltpu.roll(base, r * channels, 1) if r else base).astype(BF16)
                 for dx in range(3):
-                    taps_middle[number][r * channels : (r + 1) * channels, dx * inner : (dx + 1) * inner] = moved[
-                        dx * channels : (dx + 1) * channels, :inner
-                    ]
+                    at = (dx * chunk + r) * channels
+                    taps_middle[number][at : at + channels, :] = moved[dx * channels : (dx + 1) * channels, :inner]
         inner = (rows + 2) * channels
         padded = -(-inner // 128) * 128
         base = tap_rows(lambda n: last_ref[n].astype(F32), padded)
@@ -168,14 +184,17 @@
             ]
             hidden = silu(dot(taps_first[...], jnp.concatenate(stacked, axis=1).astype(BF16)))
             for number in range(middle):
-                stacked = [shifted(hidden[:, g * width : (g + 1) * width]).astype(BF16) for g in range(group)]
-                hidden = silu(dot(taps_middle[number][...], jnp.concatenate(stacked, axis=1)))
-            parts = dot(taps_last[...], hidden.astype(BF16))
+                chunk = chunks[number]
+                count = hidden.shape[0] // channels - 2
+                hidden = hidden.astype(BF16)
+                parts = [
+                    gathered(dot(taps_middle[number][...], hidden[r * channels : (r + chunk + 2) * channels]), width)
+                    for r in range(0, count, chunk)
+                ]
+                hidden = silu(jnp.concatenate(parts, axis=0))
+            change = gathered(dot(taps_last[...], hidden.astype(BF16)), width)
             for g in range(group):
-                part = parts[:, g * width : (g + 1) * width]
-                change = part[block : 2 * block] + pltpu.roll(part[:block], 1, 1)
-                change = change + pltpu.roll(part[2 * block :], width - 1, 1)
-                forecasts.append(own[g] + change)
+                forecasts.append(own[g] + change[:, g * width : (g + 1) * width])
 
         per_field = []
         for f in range(fields):
@@ -206,9 +225,9 @@
     for s in range(3):
         onehot[s] = jnp.where(spot == read - s * span, 1.0, 0.0).astype(BF16)
     obs_weight = jnp.exp(-0.25 * class_ref[...].astype(F32)) / variance_ref[...]
-    eye_row = lax.broadcasted_iota(jnp.int32, (ensemble, ensemble), 0)
-    eye_col = lax.broadcasted_iota(jnp.int32, (ensemble, ensemble), 1)
-    identity = jnp.where(eye_row == eye_col, 1.0, 0.0).astype(F32)
+    eye_row = lax.broadcasted_iota(jnp.int32, (ensemble, 2 * ensemble), 0)
+    eye_col = lax.broadcasted_iota(jnp.int32, (ensemble, 2 * ensemble), 1)
+    identity = jnp.where((eye_row == eye_col) | (eye_row + ensemble == eye_col), 1.0, 0.0).astype(F32)
 
     def neighbour(s):
         blocks = [inbox[s, half, k].astype(F32) for k in range(n_member) for half in range(halves)]
@@ -236,12 +255,12 @@
     heavy_high, heavy_low = split(obs_weight * obs_anom)
     gram = (ensemble - 1.0) * identity + lax.dot_general(
         jnp.concatenate([anom_high, anom_low, anom_high], axis=1),
-        jnp.concatenate([heavy_high, heavy_high, heavy_low], axis=1),
+        jnp.concatenate([jnp.concatenate([heavy_high, heavy_high, heavy_low], axis=1)] * 2, axis=0),
         (((1,), (1,)), ((), ())),
         preferred_element_type=F32,
     )
     residual = jnp.sum(obs_anom * (obs_weight * (observed_ref[...] - obs_mean)), axis=1, keepdims=True)
-    norm_scale = jnp.sqrt(jnp.sum(gram * gram, keepdims=True))
+    norm_scale = jnp.sqrt(0.5 * jnp.sum(gram * gram, keepdims=True))
     iterate_y = gram / norm_scale
     iterate_z = 1.5 * identity - 0.5 * iterate_y
     iterate_y = dot_split(iterate_y, iterate_z)
@@ -324,8 +343,13 @@
         observation_rows[0],
         loc_class[0],
     )
-    halves = 2 if members % 2 == 0 and (fields * members // 2) % 16 == 0 else 1
-    sizes = (n_member, n_tile, members, fields, rows, width, channels, depth, kept, lanes, halves)
+    halves = 1
+    chunks = []
+    for n in range(middle):
+        out_rows = rows + 2 * (depth - 2 - n)
+        most = max(1, 256 // channels - 2)
+        chunks.append(max(c for c in range(1, out_rows + 1) if out_rows % c == 0 and c <= most))
+    sizes = (n_member, n_tile, members, fields, rows, width, channels, depth, kept, lanes, halves, chunks)
     vmem = pl.BlockSpec(memory_space=pltpu.VMEM)
     packet = (fields * members, width)
     out = pl.pallas_call(
@@ -337,9 +361,7 @@
             *[pltpu.VMEM(v.shape, v.dtype) for v in operands],
             pltpu.VMEM((first_rows * channels, count), BF16),
             *[
-                pltpu.VMEM(
-                    ((rows + 2 * (depth - 2 - n)) * channels, 3 * (rows + 2 * (depth - 1 - n)) * channels), BF16
-                )
+                pltpu.VMEM((3 * chunks[n] * channels, (chunks[n] + 2) * channels), BF16)
                 for n in range(middle)
             ],
             pltpu.VMEM((3 * block, (rows + 2) * channels), BF16),

time: 27.6 us -> 25.6 us (0.928)
  Pallas kernels: 26.8 us -> 24.8 us
    pallas_call x1, Pallas kernels: 26.8 us -> 24.8 us  [local(): pl.pallas_call(functools.partial(kernel, sizes), out_shape=pltpu.VMEM((me...]
where the time goes in v4:
time: 25.6 us; the launch traced here: 25.5 us
  Pallas kernels  24.8 us (97%)
  local copies, waits for them, and re-layouts  0.63 us (2%)
    pallas_call x1, Pallas kernels, local(): pl.pallas_call(functools.partial(kernel, sizes), out_shape=pltpu.VMEM((me...  24.8 us
    unnamed x1, local copies, waits for them, and re-layouts  0.63 us

profile of v4, /device:TPU:0, one launch (start us, length us, event | category | flops | bytes accessed | tf_op | source)
XLA Modules:
  0.0 25.5 jit_solution(5019491364353507236)
XLA Ops:
  0.0 24.8 %shard_map.91 = bf16[8,32,128]{2,1,0:T(8,128)(2,1)S(1)} custom-call(bf16[8,32,128]{2,1,0:T(8,128)(2,1)} %bitcast.17, bf16[36,3072]{1,0:T(8,128)(2,1)} %constant.2.clone.refs_1_, bf16[9,4,32]{2,1,0:T(4,128)(2,1)} %bitcast.18, bf16[9,32,32]{2,1,0:T(8,128)(2,1)} %bitcast.16, bf16[9,4,32]{2,1,0:T(4,128)(2,1)} %bitcast.19, f32[1,512]{1,0:T(1,128)} %bitcast.20, ...), custom_call_target="tpu_custom_call" | custom-call | tf_op jit(solution)/shard_map/pallas_call | solution.py:355
  24.8 0.6 %copy.11 = bf16[8,4,8,128]{3,2,1,0:T(8,128)(2,1)} copy(bf16[8,4,8,128]{3,2,1,0:T(8,128)(2,1)S(1)} %bitcast.15) | data formatting | bytes 131072

commit v5 on v4

--- a/solution.py
+++ b/solution.py
@@ -85,8 +85,9 @@
     ) = fetched
     taps_first, taps_middle, refs = refs[0], refs[1 : 1 + middle], refs[1 + middle :]
     (
-        taps_last, onehot, halo_out, halo_in, outbox, inbox, back_out, back_in, fetch_sem,
-        halo_send, halo_recv, fore_send, fore_recv, back_send, back_recv,
+        taps_last, onehot, halo_out, halo_in, obs_all, outbox, inbox, sums_out, sums_in, back_out, back_in,
+        fetch_sem, halo_send, halo_recv, obs_send, obs_recv, fore_send, fore_recv, sums_send, sums_recv,
+        back_send, back_recv,
     ) = refs
     fetches = [
         pltpu.make_async_copy(source, target, fetch_sem.at[n])
@@ -110,7 +111,7 @@
         return wrapped(me + shift, n_member) if shift else me
 
     barrier = pltpu.get_barrier_semaphore()
-    peers = [(i, d) for d in (1, -1, 0) for i in range(n_member) if (i, d) != (0, 0)]
+    peers = [(0, 1), (0, -1)] + [(i, 0) for i in range(1, n_member)]
     for i, d in peers:
         pl.semaphore_signal(barrier, inc=1, device_id=(member_at(i), tile_at(d)), device_id_type=MESH)
 
@@ -136,9 +137,27 @@
         copy.start()
         halo_copies.append(copy)
 
+    for fetch in fetches[1:]:
+        fetch.wait()
+    obs_count = rows_ref.shape[1]
+    obs_weight = jnp.exp(-0.25 * class_ref[...].astype(F32)) / variance_ref[...]
+    obs_all[1] = jnp.concatenate(
+        [rows_ref[...].astype(F32), obs_weight, observed_ref[...], jnp.zeros((5, obs_count), F32)], axis=0
+    )
+    obs_copies = []
+    for side, d in ((0, 1), (2, -1)):
+        copy = pltpu.make_async_remote_copy(
+            src_ref=obs_all.at[1],
+            dst_ref=obs_all.at[side],
+            send_sem=obs_send.at[side],
+            recv_sem=obs_recv.at[side],
+            device_id=(me, tile_at(d)),
+            device_id_type=MESH,
+        )
+        copy.start()
+        obs_copies.append(copy)
+
     with jax.named_scope("taps"):
-        for fetch in fetches[1:]:
-            fetch.wait()
         first_taps = jnp.concatenate([first_ref[n].astype(F32) for n in range(9)], axis=0).astype(BF16)
         wide = lax.dot_general(
             first_taps, spread_ref[...], (((0,), (0,)), ((), ())), preferred_element_type=F32
@@ -203,63 +222,83 @@
         for r in range(rows):
             outbox[half, r] = jnp.concatenate([cube[r] for cube in per_field], axis=0).astype(BF16)
 
-        for s in (0, 2, 1):
-            for i in range(n_member):
-                if s == 1 and i == 0:
-                    continue
-                target = member_at(i)
-                copy = pltpu.make_async_remote_copy(
-                    src_ref=outbox.at[half, target],
-                    dst_ref=inbox.at[s, half, me],
-                    send_sem=fore_send.at[s, half, i],
-                    recv_sem=fore_recv.at[s, half, i],
-                    device_id=(target, tile_at(1 - s)),
-                    device_id_type=MESH,
-                )
-                copy.start()
-                fore_copies[s, half, i] = copy
-        inbox[1, half, me] = outbox[half, me]
-
-    read = rows_ref[...]
-    spot = lax.broadcasted_iota(jnp.int32, (span, read.shape[1]), 0)
-    for s in range(3):
-        onehot[s] = jnp.where(spot == read - s * span, 1.0, 0.0).astype(BF16)
-    obs_weight = jnp.exp(-0.25 * class_ref[...].astype(F32)) / variance_ref[...]
+        for i in range(1, n_member):
+            target = member_at(i)
+            copy = pltpu.make_async_remote_copy(
+                src_ref=outbox.at[half, target],
+                dst_ref=inbox.at[half, me],
+                send_sem=fore_send.at[half, i],
+                recv_sem=fore_recv.at[half, i],
+                device_id=(target, tile),
+                device_id_type=MESH,
+            )
+            copy.start()
+            fore_copies[half, i] = copy
+        inbox[half, me] = outbox[half, me]
+
+    for copy in obs_copies:
+        copy.wait_recv()
+    spot = lax.broadcasted_iota(jnp.int32, (span, obs_count), 0).astype(F32)
+    for slot in range(3):
+        read = obs_all[slot][0:1] - float((2 - slot) * span)
+        onehot[slot] = jnp.where(spot == read, 1.0, 0.0).astype(BF16)
     eye_row = lax.broadcasted_iota(jnp.int32, (ensemble, 2 * ensemble), 0)
     eye_col = lax.broadcasted_iota(jnp.int32, (ensemble, 2 * ensemble), 1)
     identity = jnp.where((eye_row == eye_col) | (eye_row + ensemble == eye_col), 1.0, 0.0).astype(F32)
 
-    def neighbour(s):
-        blocks = [inbox[s, half, k].astype(F32) for k in range(n_member) for half in range(halves)]
-        columns = [
-            jnp.concatenate([b[f * share : (f + 1) * share] for b in blocks], axis=0) for f in range(fields)
-        ]
-        return jnp.concatenate(columns, axis=1)
-
-    obs_ens = None
-    back = None
-    for s in (1, 0, 2):
-        for half in range(halves):
-            for i in range(n_member):
-                if (s, half, i) in fore_copies:
-                    fore_copies[s, half, i].wait_recv()
-        values = neighbour(s)
-        if s == 1:
-            back = values
-        part = dot(values.astype(BF16), onehot[s])
-        obs_ens = part if obs_ens is None else obs_ens + part
-
-    obs_mean = jnp.sum(obs_ens, axis=0, keepdims=True) / ensemble
-    obs_anom = obs_ens - obs_mean
-    anom_high, anom_low = split(obs_anom)
-    heavy_high, heavy_low = split(obs_weight * obs_anom)
-    gram = (ensemble - 1.0) * identity + lax.dot_general(
-        jnp.concatenate([anom_high, anom_low, anom_high], axis=1),
-        jnp.concatenate([jnp.concatenate([heavy_high, heavy_high, heavy_low], axis=1)] * 2, axis=0),
-        (((1,), (1,)), ((), ())),
-        preferred_element_type=F32,
+    left = eye_col < ensemble
+
+    for copy in fore_copies.values():
+        copy.wait_recv()
+    blocks = [inbox[half, k].astype(F32) for k in range(n_member) for half in range(halves)]
+    columns = [jnp.concatenate([b[f * share : (f + 1) * share] for b in blocks], axis=0) for f in range(fields)]
+    back = jnp.concatenate(columns, axis=1)
+    back_low = back.astype(BF16)
+
+    def partial_sums(slot):
+        given = obs_all[slot]
+        obs_ens = dot(back_low, onehot[slot])
+        obs_mean = jnp.sum(obs_ens, axis=0, keepdims=True) / ensemble
+        obs_anom = obs_ens - obs_mean
+        misfit = jnp.broadcast_to(given[2:3] - obs_mean, (8, obs_count))
+        high, low = split(jnp.concatenate([obs_anom, misfit], axis=0))
+        heavy_high, heavy_low = split(given[1:2] * obs_anom)
+        heavy = jnp.concatenate([heavy_high, heavy_high, heavy_low], axis=1)
+        total = lax.dot_general(
+            jnp.concatenate([high, low, high], axis=1),
+            jnp.concatenate([heavy, heavy], axis=0),
+            (((1,), (1,)), ((), ())),
+            preferred_element_type=F32,
+        )
+        middle_row = ensemble // 2
+        folded = jnp.where(left[:middle_row], total[:middle_row], total[middle_row:ensemble])
+        return jnp.concatenate([folded, total[ensemble:]], axis=0)
+
+    sums_copies = []
+    for side, d in ((0, -1), (2, 1)):
+        sums_out[side // 2] = partial_sums(side)
+        copy = pltpu.make_async_remote_copy(
+            src_ref=sums_out.at[side // 2],
+            dst_ref=sums_in.at[side // 2],
+            send_sem=sums_send.at[side // 2],
+            recv_sem=sums_recv.at[side // 2],
+            device_id=(me, tile_at(d)),
+            device_id_type=MESH,
+        )
+        copy.start()
+        sums_copies.append(copy)
+    sums = partial_sums(1)
+    back_mean = jnp.sum(back, axis=0, keepdims=True) / ensemble
+    back_anom = back - back_mean
+    for copy in sums_copies:
+        copy.wait_recv()
+    sums = sums + sums_in[0] + sums_in[1]
+    middle_row = ensemble // 2
+    folded, residual = sums[:middle_row], sums[middle_row : middle_row + 1]
+    turned = pltpu.roll(folded, ensemble, 1)
+    gram = (ensemble - 1.0) * identity + jnp.concatenate(
+        [jnp.where(left[:middle_row], folded, turned), jnp.where(left[:middle_row], turned, folded)], axis=0
     )
-    residual = jnp.sum(obs_anom * (obs_weight * (observed_ref[...] - obs_mean)), axis=1, keepdims=True)
     norm_scale = jnp.sqrt(0.5 * jnp.sum(gram * gram, keepdims=True))
     iterate_y = gram / norm_scale
     iterate_z = 1.5 * identity - 0.5 * iterate_y
@@ -270,10 +309,8 @@
             iterate_y = dot_split(iterate_y, factor)
         iterate_z = dot_split(factor, iterate_z)
     root_inv = iterate_z / jnp.sqrt(norm_scale)
-    back_mean = jnp.sum(back, axis=0, keepdims=True) / ensemble
-    back_anom = back - back_mean
-    both = dot_split(root_inv, jnp.concatenate([back_anom, jnp.broadcast_to(residual, (ensemble, 128))], axis=1))
-    moved, pull = both[:, :span], both[:, span : span + 1]
+    moved = dot_split(root_inv, back_anom)
+    pull = 0.5 * jnp.sum(root_inv * residual, axis=1, keepdims=True)
     shift = back_mean + jnp.sum(pull * moved, axis=0, keepdims=True)
     analysed = shift + (ensemble - 1.0) ** 0.5 * moved
 
@@ -298,7 +335,7 @@
     back_in[me] = back_out[me]
     for copy in halo_copies:
         copy.wait_send()
-    for copy in fore_copies.values():
+    for copy in (*obs_copies, *fore_copies.values(), *sums_copies):
         copy.wait_send()
     for copy in back_copies:
         copy.wait_recv()
@@ -325,6 +362,7 @@
     while fields * kept % 16:
         kept += 1
     assert kept <= rows
+    ensemble = n_member * members
     block = fields * rows
     first_rows = rows + 2 * (depth - 1)
     count = 3 * (block + 2 * fields * kept)
@@ -368,15 +406,22 @@
             pltpu.VMEM((3, span, obs), BF16),
             pltpu.VMEM((2, members, fields * kept, width), BF16),
             pltpu.VMEM((2, members, fields * kept, width), BF16),
+            pltpu.VMEM((3, 8, obs), F32),
             pltpu.VMEM((halves, n_member, fields * members // halves, width), BF16),
-            pltpu.VMEM((3, halves, n_member, fields * members // halves, width), BF16),
+            pltpu.VMEM((halves, n_member, fields * members // halves, width), BF16),
+            pltpu.VMEM((2, ensemble // 2 + 8, 2 * ensemble), F32),
+            pltpu.VMEM((2, ensemble // 2 + 8, 2 * ensemble), F32),
             pltpu.VMEM((n_member, *packet), BF16),
             pltpu.VMEM((n_member, *packet), BF16),
             pltpu.SemaphoreType.DMA((len(operands),)),
             pltpu.SemaphoreType.DMA((2,)),
             pltpu.SemaphoreType.DMA((2,)),
-            pltpu.SemaphoreType.DMA((3, halves, n_member)),
-            pltpu.SemaphoreType.DMA((3, halves, n_member)),
+            pltpu.SemaphoreType.DMA((3,)),
+            pltpu.SemaphoreType.DMA((3,)),
+            pltpu.SemaphoreType.DMA((halves, n_member)),
+            pltpu.SemaphoreType.DMA((halves, n_member)),
+            pltpu.SemaphoreType.DMA((2,)),
+            pltpu.SemaphoreType.DMA((2,)),
             pltpu.SemaphoreType.DMA((n_member,)),
             pltpu.SemaphoreType.DMA((n_member,)),
         ],

time: 25.6 us -> 25.8 us (level)
  no operation moved by 1% of the time
where the time goes in v5:
time: 25.8 us; the launch traced here: 25.7 us
  Pallas kernels  25 us (97%)
  local copies, waits for them, and re-layouts  0.63 us (2%)
    pallas_call x1, Pallas kernels, local(): pl.pallas_call(functools.partial(kernel, sizes), out_shape=pltpu.VMEM((me...  25 us
    unnamed x1, local copies, waits for them, and re-layouts  0.63 us

profile of v5, /device:TPU:0, one launch (start us, length us, event | category | flops | bytes accessed | tf_op | source)
XLA Modules:
  0.0 25.7 jit_solution(13807172074195564098)
XLA Ops:
  0.0 25.0 %shard_map.91 = bf16[8,32,128]{2,1,0:T(8,128)(2,1)S(1)} custom-call(bf16[8,32,128]{2,1,0:T(8,128)(2,1)} %bitcast.17, bf16[36,3072]{1,0:T(8,128)(2,1)} %constant.2.clone.refs_1_, bf16[9,4,32]{2,1,0:T(4,128)(2,1)} %bitcast.18, bf16[9,32,32]{2,1,0:T(8,128)(2,1)} %bitcast.16, bf16[9,4,32]{2,1,0:T(4,128)(2,1)} %bitcast.19, f32[1,512]{1,0:T(1,128)} %bitcast.20, ...), custom_call_target="tpu_custom_call" | custom-call | tf_op jit(solution)/shard_map/pallas_call | solution.py:393
  25.0 0.6 %copy.11 = bf16[8,4,8,128]{3,2,1,0:T(8,128)(2,1)} copy(bf16[8,4,8,128]{3,2,1,0:T(8,128)(2,1)S(1)} %bitcast.15) | data formatting | bytes 131072

commit v6 on v4

--- a/solution.py
+++ b/solution.py
@@ -85,7 +85,7 @@
     ) = fetched
     taps_first, taps_middle, refs = refs[0], refs[1 : 1 + middle], refs[1 + middle :]
     (
-        taps_last, onehot, halo_out, halo_in, outbox, inbox, back_out, back_in, fetch_sem,
+        taps_last, mixed, onehot, halo_out, halo_in, outbox, inbox, back_out, back_in, fetch_sem,
         halo_send, halo_recv, fore_send, fore_recv, back_send, back_recv,
     ) = refs
     fetches = [
@@ -174,34 +174,37 @@
     group = 2 if share % 2 == 0 else 1
     fore_copies = {}
     for half in range(halves):
-        forecasts = []
-        for start in range(half * share, (half + 1) * share, group):
-            ids = range(start, start + group)
-            own = [state_ref[m].astype(F32) for m in ids]
+        groups = [range(start, start + group) for start in range(half * share, (half + 1) * share, group)]
+        hidden = []
+        for ids in groups:
             stacked = [
-                shifted(jnp.concatenate([halo_in[0, m].astype(F32), own[g], halo_in[1, m].astype(F32)], axis=0))
-                for g, m in enumerate(ids)
+                shifted(jnp.concatenate([halo_in[0, m], state_ref[m], halo_in[1, m]], axis=0).astype(F32))
+                for m in ids
             ]
-            hidden = silu(dot(taps_first[...], jnp.concatenate(stacked, axis=1).astype(BF16)))
-            for number in range(middle):
-                chunk = chunks[number]
-                count = hidden.shape[0] // channels - 2
-                hidden = hidden.astype(BF16)
-                parts = [
-                    gathered(dot(taps_middle[number][...], hidden[r * channels : (r + chunk + 2) * channels]), width)
-                    for r in range(0, count, chunk)
-                ]
-                hidden = silu(jnp.concatenate(parts, axis=0))
-            change = gathered(dot(taps_last[...], hidden.astype(BF16)), width)
-            for g in range(group):
-                forecasts.append(own[g] + change[:, g * width : (g + 1) * width])
-
-        per_field = []
-        for f in range(fields):
-            cube = jnp.stack([v[f * rows : (f + 1) * rows] for v in forecasts], axis=0)
-            per_field.append(jnp.transpose(cube, (1, 0, 2)))
+            hidden.append(silu(dot(taps_first[...], jnp.concatenate(stacked, axis=1).astype(BF16))).astype(BF16))
+        for number in range(middle):
+            chunk = chunks[number]
+            count = hidden[0].shape[0] // channels - 2
+            latest = []
+            for before in hidden:
+                parts = []
+                for r in range(0, count, chunk):
+                    product = dot(taps_middle[number][...], before[r * channels : (r + chunk + 2) * channels])
+                    parts.append(silu(gathered(product, width)).astype(BF16))
+                latest.append(jnp.concatenate(parts, axis=0))
+            hidden = latest
+        for ids, before in zip(groups, hidden):
+            change = gathered(dot(taps_last[...], before), width)
+            for g, m in enumerate(ids):
+                mixed[m * block : (m + 1) * block, :] = (
+                    state_ref[m].astype(F32) + change[:, g * width : (g + 1) * width]
+                )
+
         for r in range(rows):
-            outbox[half, r] = jnp.concatenate([cube[r] for cube in per_field], axis=0).astype(BF16)
+            outbox[half, r] = jnp.concatenate(
+                [mixed[pl.ds(half * share * block + f * rows + r, share, stride=block), :] for f in range(fields)],
+                axis=0,
+            ).astype(BF16)
 
         for s in (0, 2, 1):
             for i in range(n_member):
@@ -302,13 +305,13 @@
         copy.wait_send()
     for copy in back_copies:
         copy.wait_recv()
-    landed = [back_in[r].astype(F32) for r in range(rows)]
-    per_field = []
-    for f in range(fields):
-        cube = jnp.stack([v[f * members : (f + 1) * members] for v in landed], axis=0)
-        per_field.append(jnp.transpose(cube, (1, 0, 2)))
+    pack = fields * members
+    for r in range(rows):
+        mixed[r * pack : (r + 1) * pack, :] = back_in[r].astype(F32)
     for m in range(members):
-        out_ref[m] = jnp.concatenate([cube[m] for cube in per_field], axis=0).astype(BF16)
+        out_ref[m] = jnp.concatenate(
+            [mixed[pl.ds(f * members + m, rows, stride=pack), :] for f in range(fields)], axis=0
+        ).astype(BF16)
     for copy in back_copies:
         copy.wait_send()
 
@@ -365,6 +368,7 @@
                 for n in range(middle)
             ],
             pltpu.VMEM((3 * block, (rows + 2) * channels), BF16),
+            pltpu.VMEM((members * block, width), F32),
             pltpu.VMEM((3, span, obs), BF16),
             pltpu.VMEM((2, members, fields * kept, width), BF16),
             pltpu.VMEM((2, members, fields * kept, width), BF16),

time: 25.6 us -> 24.6 us (0.961)
  Pallas kernels: 24.8 us -> 23.8 us
    pallas_call x1, Pallas kernels: 24.8 us -> 23.8 us  [local(): pl.pallas_call(functools.partial(kernel, sizes), out_shape=pltpu.VMEM((me...]
where the time goes in v6:
time: 24.6 us; the launch traced here: 24.5 us
  Pallas kernels  23.8 us (97%)
  local copies, waits for them, and re-layouts  0.63 us (3%)
    pallas_call x1, Pallas kernels, local(): pl.pallas_call(functools.partial(kernel, sizes), out_shape=pltpu.VMEM((me...  23.8 us
    unnamed x1, local copies, waits for them, and re-layouts  0.63 us

profile of v6, /device:TPU:0, one launch (start us, length us, event | category | flops | bytes accessed | tf_op | source)
XLA Modules:
  0.0 24.5 jit_solution(15758648158846825789)
XLA Ops:
  0.0 23.8 %shard_map.91 = bf16[8,32,128]{2,1,0:T(8,128)(2,1)S(1)} custom-call(bf16[8,32,128]{2,1,0:T(8,128)(2,1)} %bitcast.17, bf16[36,3072]{1,0:T(8,128)(2,1)} %constant.2.clone.refs_1_, bf16[9,4,32]{2,1,0:T(4,128)(2,1)} %bitcast.18, bf16[9,32,32]{2,1,0:T(8,128)(2,1)} %bitcast.16, bf16[9,4,32]{2,1,0:T(4,128)(2,1)} %bitcast.19, f32[1,512]{1,0:T(1,128)} %bitcast.20, ...), custom_call_target="tpu_custom_call" | custom-call | tf_op jit(solution)/shard_map/pallas_call | solution.py:358
  23.8 0.6 %copy.11 = bf16[8,4,8,128]{3,2,1,0:T(8,128)(2,1)} copy(bf16[8,4,8,128]{3,2,1,0:T(8,128)(2,1)S(1)} %bitcast.15) | data formatting | bytes 131072

commit v7 on v6

--- a/solution.py
+++ b/solution.py
@@ -19,18 +19,32 @@
     return half + half * jnp.tanh(half)
 
 
-def first_selector(fields, rows, kept, halo, out_rows, lanes):
-    where = [(f, halo - kept + q) for f in range(fields) for q in range(kept)]
-    where += [(f, halo + r) for f in range(fields) for r in range(rows)]
-    where += [(f, halo + rows + q) for f in range(fields) for q in range(kept)]
-    count = len(where)
-    spread = np.zeros((3, 3, fields, out_rows, lanes), np.float32)
+def first_selector(fields, where, out_rows, lanes):
+    spread = np.zeros((3, 3, fields, len(out_rows), lanes), np.float32)
     for dx in range(3):
         for k, (f, row) in enumerate(where):
-            for r in range(out_rows):
+            for n, r in enumerate(out_rows):
                 if 0 <= row - r <= 2:
-                    spread[row - r, dx, f, r, dx * count + k] = 1
-    return spread.reshape(9 * fields, out_rows * lanes)
+                    spread[row - r, dx, f, n, dx * len(where) + k] = 1
+    return spread.reshape(9 * fields, len(out_rows) * lanes)
+
+
+def middle_layer(taps, hidden, chunk, channels, width):
+    count = hidden.shape[0] // channels - 2
+    parts = [
+        silu(gathered(dot(taps, hidden[r * channels : (r + chunk + 2) * channels]), width)).astype(BF16)
+        for r in range(0, count, chunk)
+    ]
+    return jnp.concatenate(parts, axis=0)
+
+
+def spread_middle(taps, base, chunk, channels):
+    inner = (chunk + 2) * channels
+    for r in range(chunk):
+        moved = (pltpu.roll(base, r * channels, 1) if r else base).astype(BF16)
+        for dx in range(3):
+            at = (dx * chunk + r) * channels
+            taps[at : at + channels, :] = moved[dx * channels : (dx + 1) * channels, :inner]
 
 
 def dot(a, b):
@@ -77,13 +91,15 @@
 
 def kernel(sizes, *refs):
     n_member, n_tile, members, fields, rows, width, channels, depth, kept, lanes, halves, chunks = sizes
+    edge_lanes, own_lanes = lanes
     middle = depth - 2
     sources, out_ref, refs = refs[:9], refs[9], refs[10:]
     fetched, refs = refs[:9], refs[9:]
     (
         state_ref, spread_ref, first_ref, middle_ref, last_ref, observed_ref, variance_ref, rows_ref, class_ref,
     ) = fetched
-    taps_first, taps_middle, refs = refs[0], refs[1 : 1 + middle], refs[1 + middle :]
+    taps_first, taps_own, taps_edge, refs = refs[0], refs[1], refs[2], refs[3:]
+    taps_middle, refs = refs[:middle], refs[middle:]
     (
         taps_last, mixed, onehot, halo_out, halo_in, outbox, inbox, back_out, back_in, fetch_sem,
         halo_send, halo_recv, fore_send, fore_recv, back_send, back_recv,
@@ -143,20 +159,19 @@
         wide = lax.dot_general(
             first_taps, spread_ref[...], (((0,), (0,)), ((), ())), preferred_element_type=F32
         ).astype(BF16)
-        first_rows = rows + 2 * (depth - 1)
         count = taps_first.shape[1]
-        for r in range(first_rows):
-            taps_first[r * channels : (r + 1) * channels, :] = wide[:, r * lanes : r * lanes + count]
+        for r in range(2 * depth):
+            taps_first[r * channels : (r + 1) * channels, :] = wide[:, r * edge_lanes : r * edge_lanes + count]
+        begin = 2 * depth * edge_lanes
+        count = taps_own.shape[1]
+        for r in range(rows - 2):
+            taps_own[r * channels : (r + 1) * channels, :] = wide[:, begin + r * own_lanes : begin + r * own_lanes + count]
         for number in range(middle):
-            chunk = chunks[number]
-            inner = (chunk + 2) * channels
-            padded = -(-inner // 128) * 128
-            base = tap_rows(lambda n: middle_ref[9 * number + n].astype(F32), padded)
-            for r in range(chunk):
-                moved = (pltpu.roll(base, r * channels, 1) if r else base).astype(BF16)
-                for dx in range(3):
-                    at = (dx * chunk + r) * channels
-                    taps_middle[number][at : at + channels, :] = moved[dx * channels : (dx + 1) * channels, :inner]
+            chunk = max(chunks[number], depth)
+            base = tap_rows(lambda n: middle_ref[9 * number + n].astype(F32), -(-(chunk + 2) * channels // 128) * 128)
+            spread_middle(taps_middle[number], base, chunks[number], channels)
+            if number == 0:
+                spread_middle(taps_edge, base, depth, channels)
         inner = (rows + 2) * channels
         padded = -(-inner // 128) * 128
         base = tap_rows(lambda n: last_ref[n].astype(F32), padded)
@@ -167,32 +182,38 @@
             total = total + jnp.where(row_of == r, pltpu.roll(base, r * channels, 1), 0.0)
         taps_last[...] = total.astype(BF16)[:, :inner]
 
+    share = members // halves
+    group = 2 if share % 2 == 0 else 1
+    groups = [range(start, start + group) for start in range(0, members, group)]
+
+    own_first = []
+    for ids in groups:
+        stacked = [shifted(state_ref[m].astype(F32)) for m in ids]
+        own_first.append(silu(dot(taps_own[...], jnp.concatenate(stacked, axis=1).astype(BF16))).astype(BF16))
+    own_second = [middle_layer(taps_middle[0][...], v, chunks[0], channels, width) for v in own_first]
+
     for copy in halo_copies:
         copy.wait_recv()
 
-    share = members // halves
-    group = 2 if share % 2 == 0 else 1
     fore_copies = {}
     for half in range(halves):
-        groups = [range(start, start + group) for start in range(half * share, (half + 1) * share, group)]
-        hidden = []
+        edge_first = []
         for ids in groups:
             stacked = [
                 shifted(jnp.concatenate([halo_in[0, m], state_ref[m], halo_in[1, m]], axis=0).astype(F32))
                 for m in ids
             ]
-            hidden.append(silu(dot(taps_first[...], jnp.concatenate(stacked, axis=1).astype(BF16))).astype(BF16))
-        for number in range(middle):
-            chunk = chunks[number]
-            count = hidden[0].shape[0] // channels - 2
-            latest = []
-            for before in hidden:
-                parts = []
-                for r in range(0, count, chunk):
-                    product = dot(taps_middle[number][...], before[r * channels : (r + chunk + 2) * channels])
-                    parts.append(silu(gathered(product, width)).astype(BF16))
-                latest.append(jnp.concatenate(parts, axis=0))
-            hidden = latest
+            edge_first.append(silu(dot(taps_first[...], jnp.concatenate(stacked, axis=1).astype(BF16))).astype(BF16))
+        hidden = []
+        cut = depth * channels
+        for edge, own, second in zip(edge_first, own_first, own_second):
+            above = jnp.concatenate([edge[:cut], own[: 2 * channels]], axis=0)
+            below = jnp.concatenate([own[(rows - 4) * channels :], edge[cut:]], axis=0)
+            above = middle_layer(taps_edge[...], above, depth, channels, width)
+            below = middle_layer(taps_edge[...], below, depth, channels, width)
+            hidden.append(jnp.concatenate([above, second, below], axis=0))
+        for number in range(1, middle):
+            hidden = [middle_layer(taps_middle[number][...], v, chunks[number], channels, width) for v in hidden]
         for ids, before in zip(groups, hidden):
             change = gathered(dot(taps_last[...], before), width)
             for g, m in enumerate(ids):
@@ -327,14 +348,27 @@
     kept = depth
     while fields * kept % 16:
         kept += 1
-    assert kept <= rows
+    assert kept <= rows and rows > 4
     block = fields * rows
     first_rows = rows + 2 * (depth - 1)
-    count = 3 * (block + 2 * fields * kept)
-    lanes = -(-count // 128) * 128
     obs = observations.shape[2]
     span = fields * width
-    spread = jnp.asarray(first_selector(fields, rows, kept, depth, first_rows, lanes), BF16)
+    whole_lines = [(f, depth - kept + q) for f in range(fields) for q in range(kept)]
+    own_lines = [(f, depth + r) for f in range(fields) for r in range(rows)]
+    whole_lines += own_lines + [(f, depth + rows + q) for f in range(fields) for q in range(kept)]
+    own_rows = range(depth, depth + rows - 2)
+    edge_rows = [r for r in range(first_rows) if r not in own_rows]
+    lanes = tuple(-(-3 * len(lines) // 128) * 128 for lines in (whole_lines, own_lines))
+    spread = jnp.asarray(
+        np.concatenate(
+            [
+                first_selector(fields, whole_lines, edge_rows, lanes[0]),
+                first_selector(fields, own_lines, own_rows, lanes[1]),
+            ],
+            axis=1,
+        ),
+        BF16,
+    )
     operands = (
         state.reshape(members, block, width),
         spread,
@@ -349,7 +383,7 @@
     halves = 1
     chunks = []
     for n in range(middle):
-        out_rows = rows + 2 * (depth - 2 - n)
+        out_rows = rows + 2 * (depth - 2 - n) if n else rows - 4
         most = max(1, 256 // channels - 2)
         chunks.append(max(c for c in range(1, out_rows + 1) if out_rows % c == 0 and c <= most))
     sizes = (n_member, n_tile, members, fields, rows, width, channels, depth, kept, lanes, halves, chunks)
@@ -362,7 +396,9 @@
         out_specs=vmem,
         scratch_shapes=[
             *[pltpu.VMEM(v.shape, v.dtype) for v in operands],
-            pltpu.VMEM((first_rows * channels, count), BF16),
+            pltpu.VMEM((2 * depth * channels, 3 * len(whole_lines)), BF16),
+            pltpu.VMEM(((rows - 2) * channels, 3 * len(own_lines)), BF16),
+            pltpu.VMEM((3 * depth * channels, (depth + 2) * channels), BF16),
             *[
                 pltpu.VMEM((3 * chunks[n] * channels, (chunks[n] + 2) * channels), BF16)
                 for n in range(middle)

time: 24.6 us -> 24.2 us (0.984)
  Pallas kernels: 23.8 us -> 23.4 us
    pallas_call x1, Pallas kernels: 23.8 us -> 23.4 us  [local(): pl.pallas_call(functools.partial(kernel, sizes), out_shape=pltpu.VMEM((me...]
where the time goes in v7:
time: 24.2 us; the launch traced here: 24.1 us
  Pallas kernels  23.4 us (97%)
  local copies, waits for them, and re-layouts  0.63 us (3%)
    pallas_call x1, Pallas kernels, local(): pl.pallas_call(functools.partial(kernel, sizes), out_shape=pltpu.VMEM((me...  23.4 us
    unnamed x1, local copies, waits for them, and re-layouts  0.63 us

profile of v7, /device:TPU:0, one launch (start us, length us, event | category | flops | bytes accessed | tf_op | source)
XLA Modules:
  0.0 24.1 jit_solution(13635013926905659055)
XLA Ops:
  0.0 23.4 %shard_map.91 = bf16[8,32,128]{2,1,0:T(8,128)(2,1)S(1)} custom-call(bf16[8,32,128]{2,1,0:T(8,128)(2,1)} %bitcast.17, bf16[36,2304]{1,0:T(8,128)(2,1)} %constant.2.clone.refs_1_, bf16[9,4,32]{2,1,0:T(4,128)(2,1)} %bitcast.18, bf16[9,32,32]{2,1,0:T(8,128)(2,1)} %bitcast.16, bf16[9,4,32]{2,1,0:T(4,128)(2,1)} %bitcast.19, f32[1,512]{1,0:T(1,128)} %bitcast.20, ...), custom_call_target="tpu_custom_call" | custom-call | tf_op jit(solution)/shard_map/pallas_call | solution.py:392
  23.4 0.6 %copy.11 = bf16[8,4,8,128]{3,2,1,0:T(8,128)(2,1)} copy(bf16[8,4,8,128]{3,2,1,0:T(8,128)(2,1)S(1)} %bitcast.15) | data formatting | bytes 131072

commit v8 on v7

--- a/solution.py
+++ b/solution.py
@@ -195,7 +195,6 @@
     for copy in halo_copies:
         copy.wait_recv()
 
-    fore_copies = {}
     for half in range(halves):
         edge_first = []
         for ids in groups:
@@ -235,13 +234,12 @@
                 copy = pltpu.make_async_remote_copy(
                     src_ref=outbox.at[half, target],
                     dst_ref=inbox.at[s, half, me],
-                    send_sem=fore_send.at[s, half, i],
-                    recv_sem=fore_recv.at[s, half, i],
+                    send_sem=fore_send.at[s, half],
+                    recv_sem=fore_recv.at[s, half],
                     device_id=(target, tile_at(1 - s)),
                     device_id_type=MESH,
                 )
                 copy.start()
-                fore_copies[s, half, i] = copy
         inbox[1, half, me] = outbox[half, me]
 
     read = rows_ref[...]
@@ -249,6 +247,7 @@
     for s in range(3):
         onehot[s] = jnp.where(spot == read - s * span, 1.0, 0.0).astype(BF16)
     obs_weight = jnp.exp(-0.25 * class_ref[...].astype(F32)) / variance_ref[...]
+    obs_root = jnp.sqrt(obs_weight)
     eye_row = lax.broadcasted_iota(jnp.int32, (ensemble, 2 * ensemble), 0)
     eye_col = lax.broadcasted_iota(jnp.int32, (ensemble, 2 * ensemble), 1)
     identity = jnp.where((eye_row == eye_col) | (eye_row + ensemble == eye_col), 1.0, 0.0).astype(F32)
@@ -260,13 +259,15 @@
         ]
         return jnp.concatenate(columns, axis=1)
 
+    def arriving(s):
+        return n_member - 1 if s == 1 else n_member
+
     obs_ens = None
     back = None
     for s in (1, 0, 2):
         for half in range(halves):
-            for i in range(n_member):
-                if (s, half, i) in fore_copies:
-                    fore_copies[s, half, i].wait_recv()
+            packets = inbox.at[s, half, pl.ds(0, arriving(s))]
+            pltpu.make_async_copy(packets, packets, fore_recv.at[s, half]).wait()
         values = neighbour(s)
         if s == 1:
             back = values
@@ -275,14 +276,10 @@
 
     obs_mean = jnp.sum(obs_ens, axis=0, keepdims=True) / ensemble
     obs_anom = obs_ens - obs_mean
-    anom_high, anom_low = split(obs_anom)
-    heavy_high, heavy_low = split(obs_weight * obs_anom)
-    gram = (ensemble - 1.0) * identity + lax.dot_general(
-        jnp.concatenate([anom_high, anom_low, anom_high], axis=1),
-        jnp.concatenate([jnp.concatenate([heavy_high, heavy_high, heavy_low], axis=1)] * 2, axis=0),
-        (((1,), (1,)), ((), ())),
-        preferred_element_type=F32,
-    )
+    parts = jnp.concatenate(split(obs_root * obs_anom), axis=0)
+    quadrants = lax.dot_general(parts, parts, (((1,), (1,)), ((), ())), preferred_element_type=F32)
+    beside = quadrants[:ensemble] + quadrants[ensemble:]
+    gram = (ensemble - 1.0) * identity + (beside + pltpu.roll(beside, ensemble, 1))
     residual = jnp.sum(obs_anom * (obs_weight * (observed_ref[...] - obs_mean)), axis=1, keepdims=True)
     norm_scale = jnp.sqrt(0.5 * jnp.sum(gram * gram, keepdims=True))
     iterate_y = gram / norm_scale
@@ -306,26 +303,26 @@
         back_out[k] = jnp.concatenate(
             [rows_k[:, f * width : (f + 1) * width] for f in range(fields)], axis=0
         ).astype(BF16)
-    back_copies = []
     for i in range(1, n_member):
         target = member_at(i)
         copy = pltpu.make_async_remote_copy(
             src_ref=back_out.at[target],
             dst_ref=back_in.at[me],
-            send_sem=back_send.at[i],
-            recv_sem=back_recv.at[i],
+            send_sem=back_send,
+            recv_sem=back_recv,
             device_id=(target, tile),
             device_id_type=MESH,
         )
         copy.start()
-        back_copies.append(copy)
     back_in[me] = back_out[me]
     for copy in halo_copies:
         copy.wait_send()
-    for copy in fore_copies.values():
-        copy.wait_send()
-    for copy in back_copies:
-        copy.wait_recv()
+    for s in range(3):
+        for half in range(halves):
+            packets = outbox.at[half, pl.ds(0, arriving(s))]
+            pltpu.make_async_copy(packets, packets, fore_send.at[s, half]).wait()
+    packets = back_in.at[pl.ds(0, n_member - 1)]
+    pltpu.make_async_copy(packets, packets, back_recv).wait()
     pack = fields * members
     for r in range(rows):
         mixed[r * pack : (r + 1) * pack, :] = back_in[r].astype(F32)
@@ -333,8 +330,8 @@
         out_ref[m] = jnp.concatenate(
             [mixed[pl.ds(f * members + m, rows, stride=pack), :] for f in range(fields)], axis=0
         ).astype(BF16)
-    for copy in back_copies:
-        copy.wait_send()
+    packets = back_out.at[pl.ds(0, n_member - 1)]
+    pltpu.make_async_copy(packets, packets, back_send).wait()
 
 
 def local(state, first_weight, middle_weight, last_weight, observations, obs_variance, observation_rows, loc_class):
@@ -415,10 +412,10 @@
             pltpu.SemaphoreType.DMA((len(operands),)),
             pltpu.SemaphoreType.DMA((2,)),
             pltpu.SemaphoreType.DMA((2,)),
-            pltpu.SemaphoreType.DMA((3, halves, n_member)),
-            pltpu.SemaphoreType.DMA((3, halves, n_member)),
-            pltpu.SemaphoreType.DMA((n_member,)),
-            pltpu.SemaphoreType.DMA((n_member,)),
+            pltpu.SemaphoreType.DMA((3, halves)),
+            pltpu.SemaphoreType.DMA((3, halves)),
+            pltpu.SemaphoreType.DMA,
+            pltpu.SemaphoreType.DMA,
         ],
         compiler_params=pltpu.CompilerParams(
             collective_id=0, has_side_effects=True, vmem_limit_bytes=60 * 1024 * 1024

time: 24.2 us -> 23.7 us (0.979)
  Pallas kernels: 23.4 us -> 22.9 us
    pallas_call x1, Pallas kernels: 23.4 us -> 22.9 us  [local(): pl.pallas_call(functools.partial(kernel, sizes), out_shape=pltpu.VMEM((me...]
where the time goes in v8:
time: 23.7 us; the launch traced here: 23.5 us
  Pallas kernels  22.9 us (97%)
  local copies, waits for them, and re-layouts  0.63 us (3%)
    pallas_call x1, Pallas kernels, local(): pl.pallas_call(functools.partial(kernel, sizes), out_shape=pltpu.VMEM((me...  22.9 us
    unnamed x1, local copies, waits for them, and re-layouts  0.63 us

profile of v8, /device:TPU:0, one launch (start us, length us, event | category | flops | bytes accessed | tf_op | source)
XLA Modules:
  0.0 23.5 jit_solution(16876244055305696151)
XLA Ops:
  0.0 22.9 %shard_map.91 = bf16[8,32,128]{2,1,0:T(8,128)(2,1)S(1)} custom-call(bf16[8,32,128]{2,1,0:T(8,128)(2,1)} %bitcast.17, bf16[36,2304]{1,0:T(8,128)(2,1)} %constant.2.clone.refs_1_, bf16[9,4,32]{2,1,0:T(4,128)(2,1)} %bitcast.18, bf16[9,32,32]{2,1,0:T(8,128)(2,1)} %bitcast.16, bf16[9,4,32]{2,1,0:T(4,128)(2,1)} %bitcast.19, f32[1,512]{1,0:T(1,128)} %bitcast.20, ...), custom_call_target="tpu_custom_call" | custom-call | tf_op jit(solution)/shard_map/pallas_call | solution.py:389
  22.9 0.6 %copy.11 = bf16[8,4,8,128]{3,2,1,0:T(8,128)(2,1)} copy(bf16[8,4,8,128]{3,2,1,0:T(8,128)(2,1)S(1)} %bitcast.15) | data formatting | bytes 131072

commit v9 on v8

--- a/solution.py
+++ b/solution.py
@@ -56,13 +56,21 @@
     return high, (v - high.astype(F32)).astype(BF16)
 
 
+def stacked_parts(b):
+    high, low = split(b)
+    return jnp.concatenate([high, high, low, low], axis=0)
+
+
 def dot_split(a_twice, b):
+    return dot_stacked(a_twice, stacked_parts(b))
+
+
+def dot_stacked(a_twice, b_parts):
     high, low = split(a_twice)
     size = a_twice.shape[0]
     lane = lax.broadcasted_iota(jnp.int32, a_twice.shape, 1)
     mixed = jnp.where(lane < size, high.astype(F32), low.astype(F32)).astype(BF16)
-    b_high, b_low = split(b)
-    return dot(jnp.concatenate([mixed, mixed], axis=1), jnp.concatenate([b_high, b_high, b_low, b_low], axis=0))
+    return dot(jnp.concatenate([mixed, mixed], axis=1), b_parts)
 
 
 def shifted(v):
@@ -263,14 +271,14 @@
         return n_member - 1 if s == 1 else n_member
 
     obs_ens = None
-    back = None
     for s in (1, 0, 2):
         for half in range(halves):
             packets = inbox.at[s, half, pl.ds(0, arriving(s))]
             pltpu.make_async_copy(packets, packets, fore_recv.at[s, half]).wait()
         values = neighbour(s)
         if s == 1:
-            back = values
+            back_mean = jnp.sum(values, axis=0, keepdims=True) / ensemble
+            back_anom = stacked_parts(values - back_mean)
         part = dot(values.astype(BF16), onehot[s])
         obs_ens = part if obs_ens is None else obs_ens + part
 
@@ -291,10 +299,8 @@
             iterate_y = dot_split(iterate_y, factor)
         iterate_z = dot_split(factor, iterate_z)
     root_inv = iterate_z / jnp.sqrt(norm_scale)
-    back_mean = jnp.sum(back, axis=0, keepdims=True) / ensemble
-    back_anom = back - back_mean
-    both = dot_split(root_inv, jnp.concatenate([back_anom, jnp.broadcast_to(residual, (ensemble, 128))], axis=1))
-    moved, pull = both[:, :span], both[:, span : span + 1]
+    moved = dot_stacked(root_inv, back_anom)
+    pull = dot_split(root_inv, jnp.broadcast_to(residual, (ensemble, 128)))[:, :1]
     shift = back_mean + jnp.sum(pull * moved, axis=0, keepdims=True)
     analysed = shift + (ensemble - 1.0) ** 0.5 * moved
 
@@ -323,13 +329,7 @@
             pltpu.make_async_copy(packets, packets, fore_send.at[s, half]).wait()
     packets = back_in.at[pl.ds(0, n_member - 1)]
     pltpu.make_async_copy(packets, packets, back_recv).wait()
-    pack = fields * members
-    for r in range(rows):
-        mixed[r * pack : (r + 1) * pack, :] = back_in[r].astype(F32)
-    for m in range(members):
-        out_ref[m] = jnp.concatenate(
-            [mixed[pl.ds(f * members + m, rows, stride=pack), :] for f in range(fields)], axis=0
-        ).astype(BF16)
+    out_ref[...] = back_in[...]
     packets = back_out.at[pl.ds(0, n_member - 1)]
     pltpu.make_async_copy(packets, packets, back_send).wait()
 
@@ -388,7 +388,7 @@
     packet = (fields * members, width)
     out = pl.pallas_call(
         functools.partial(kernel, sizes),
-        out_shape=pltpu.VMEM((members, block, width), BF16),
+        out_shape=pltpu.VMEM((rows, *packet), BF16),
         in_specs=[pl.BlockSpec(memory_space=pltpu.HBM)] * len(operands),
         out_specs=vmem,
         scratch_shapes=[
@@ -421,7 +421,7 @@
             collective_id=0, has_side_effects=True, vmem_limit_bytes=60 * 1024 * 1024
         ),
     )(*operands)
-    return out.reshape(members, fields, rows, width)
+    return jnp.transpose(out.reshape(rows, fields, members, width), (2, 1, 0, 3))
 
 
 def solution(mesh):

time: 23.7 us -> 23.6 us (level)
    reshape x0 -> x1, local copies, waits for them, and re-layouts: none -> 0.66 us  [local(): out.reshape(rows, fields, members, width)]
    unnamed x1 -> x0, local copies, waits for them, and re-layouts: 0.63 us -> none
where the time goes in v9:
time: 23.6 us; the launch traced here: 23.4 us
  Pallas kernels  22.8 us (97%)
  local copies, waits for them, and re-layouts  0.66 us (3%)
    pallas_call x1, Pallas kernels, local(): pl.pallas_call(functools.partial(kernel, sizes), out_shape=pltpu.VMEM((ro...  22.8 us
    reshape x1, local copies, waits for them, and re-layouts, local(): out.reshape(rows, fields, members, width)  0.66 us

profile of v9, /device:TPU:0, one launch (start us, length us, event | category | flops | bytes accessed | tf_op | source)
XLA Modules:
  0.0 23.4 jit_solution(914075543911004761)
XLA Ops:
  0.0 22.8 %shard_map.91 = bf16[8,32,128]{2,1,0:T(8,128)(2,1)S(1)} custom-call(bf16[8,32,128]{2,1,0:T(8,128)(2,1)} %bitcast.20, bf16[36,2304]{1,0:T(8,128)(2,1)} %constant.2.clone.refs_1_, bf16[9,4,32]{2,1,0:T(4,128)(2,1)} %bitcast.21, bf16[9,32,32]{2,1,0:T(8,128)(2,1)} %bitcast.19, bf16[9,4,32]{2,1,0:T(4,128)(2,1)} %bitcast.22, f32[1,512]{1,0:T(1,128)} %bitcast.23, ...), custom_call_target="tpu_custom_call" | custom-call | tf_op jit(solution)/shard_map/pallas_call | solution.py:389
  22.8 0.7 %copy.12 = bf16[8,4,8,128]{3,0,1,2:T(8,128)(2,1)} copy(bf16[8,4,8,128]{3,2,1,0:T(8,128)(2,1)S(1)} %bitcast.18) | data formatting | bytes 131072 | tf_op jit(solution)/shard_map/reshape | solution.py:424

commit v10 on v9

--- a/solution.py
+++ b/solution.py
@@ -146,20 +146,6 @@
         each = [whole[f * rows : (f + 1) * rows] for f in range(fields)]
         halo_out[0, m] = jnp.concatenate([v[rows - kept :] for v in each], axis=0).astype(BF16)
         halo_out[1, m] = jnp.concatenate([v[:kept] for v in each], axis=0).astype(BF16)
-    pl.semaphore_wait(barrier, len(peers))
-    halo_copies = []
-    for side, d in ((0, 1), (1, -1)):
-        copy = pltpu.make_async_remote_copy(
-            src_ref=halo_out.at[side],
-            dst_ref=halo_in.at[side],
-            send_sem=halo_send.at[side],
-            recv_sem=halo_recv.at[side],
-            device_id=(me, tile_at(d)),
-            device_id_type=MESH,
-        )
-        copy.start()
-        halo_copies.append(copy)
-
     with jax.named_scope("taps"):
         for fetch in fetches[1:]:
             fetch.wait()
@@ -189,6 +175,20 @@
         for r in range(1, rows):
             total = total + jnp.where(row_of == r, pltpu.roll(base, r * channels, 1), 0.0)
         taps_last[...] = total.astype(BF16)[:, :inner]
+
+    pl.semaphore_wait(barrier, len(peers))
+    halo_copies = []
+    for side, d in ((0, 1), (1, -1)):
+        copy = pltpu.make_async_remote_copy(
+            src_ref=halo_out.at[side],
+            dst_ref=halo_in.at[side],
+            send_sem=halo_send.at[side],
+            recv_sem=halo_recv.at[side],
+            device_id=(me, tile_at(d)),
+            device_id_type=MESH,
+        )
+        copy.start()
+        halo_copies.append(copy)
 
     share = members // halves
     group = 2 if share % 2 == 0 else 1

time: 23.6 us -> 23.6 us (level)
  no operation moved by 1% of the time
where the time goes in v10:
time: 23.6 us; the launch traced here: 23.5 us
  Pallas kernels  22.8 us (97%)
  local copies, waits for them, and re-layouts  0.66 us (3%)
    pallas_call x1, Pallas kernels, local(): pl.pallas_call(functools.partial(kernel, sizes), out_shape=pltpu.VMEM((ro...  22.8 us
    reshape x1, local copies, waits for them, and re-layouts, local(): out.reshape(rows, fields, members, width)  0.66 us

profile of v10, /device:TPU:0, one launch (start us, length us, event | category | flops | bytes accessed | tf_op | source)
XLA Modules:
  0.0 23.5 jit_solution(6028822350548172926)
XLA Ops:
  0.0 22.8 %shard_map.91 = bf16[8,32,128]{2,1,0:T(8,128)(2,1)S(1)} custom-call(bf16[8,32,128]{2,1,0:T(8,128)(2,1)} %bitcast.20, bf16[36,2304]{1,0:T(8,128)(2,1)} %constant.2.clone.refs_1_, bf16[9,4,32]{2,1,0:T(4,128)(2,1)} %bitcast.21, bf16[9,32,32]{2,1,0:T(8,128)(2,1)} %bitcast.19, bf16[9,4,32]{2,1,0:T(4,128)(2,1)} %bitcast.22, f32[1,512]{1,0:T(1,128)} %bitcast.23, ...), custom_call_target="tpu_custom_call" | custom-call | tf_op jit(solution)/shard_map/pallas_call | solution.py:389
  22.8 0.7 %copy.12 = bf16[8,4,8,128]{3,0,1,2:T(8,128)(2,1)} copy(bf16[8,4,8,128]{3,2,1,0:T(8,128)(2,1)S(1)} %bitcast.18) | data formatting | bytes 131072 | tf_op jit(solution)/shard_map/reshape | solution.py:424
